TPU v7x, 256 devices: a whole 4x4x8 slice. The times are simulated.
256 devices in a mesh: grp: 16 (over z_lo, x, core), sp: 16 (over y, z_hi).
Axes of the slice: x: 4, y: 4, z: 8 (z_hi: 4, z_lo: 2; z = z_hi * 2 + z_lo), core: 2. Of those that a mesh axis runs over, the one named last changes fastest.
Arguments:
- img_q: bfloat16 [16, 2048, 3072], P('grp', 'sp'), may hold values from -6 to 6
- img_k: bfloat16 [16, 2048, 3072], P('grp', 'sp'), may hold values from -6 to 6
- img_v: bfloat16 [16, 2048, 3072], P('grp', 'sp'), may hold values from -6 to 6
- cond_rows: bfloat16 [16, 128, 9216], P('grp', 'sp'), may hold values from -6 to 6
- prompt_len: int32 [16], replicated, may hold values from 1 to 64, 512 in all
- ref_count: int32 [16], replicated, may hold values from 1 to 64, 512 in all
- assign: int32 [16], replicated, may hold values from 0 to 15, each once
Outputs:
- img_out: bfloat16 [16, 2048, 3072], P('grp', 'sp')
- txt_out: bfloat16 [16, 128, 3072], P('grp', 'sp')
Inputs may be any that keep to these rules, and one draw needn't show every extreme that they name: `prompt_len`: the 16 prompt lengths sum to 512. `ref_count`: the 16 reference token counts sum to 512. `assign`: every group serves exactly one request.
All inputs are finite; a program needn't handle non-finite values.
Results may differ from a plain program's by a relative error of at most 0.0048.
Values may be sent and summed in bfloat16 or wider, within the bound.
No kernel may reach another device: no remote copies, remote signals or barrier semaphores. Data moves between devices by JAX's collectives and lax.ppermute only.
A program may use at most 128 MiB of HBM per device.

v0:
```python
import math

import jax
import jax.numpy as jnp
from jax import lax
from jax.sharding import PartitionSpec as P

HD = 128


NEG_FILL = -1e30


def slot_alive(slots, owner_ref, owner_prompt, ref_slots):
    return jnp.where(slots < ref_slots, slots < owner_ref, slots - ref_slots < owner_prompt)


def block_attention(queries, keys_all, values_all, alive, head_count, head_size):
    scale = 1.0 / math.sqrt(head_size)
    total_rows = queries.shape[0]
    blocks = max(1, total_rows // 512)
    while total_rows % blocks:
        blocks = blocks - 1
    span = total_rows // blocks
    key_heads = keys_all.reshape(keys_all.shape[0], head_count, head_size)
    value_heads = values_all.reshape(values_all.shape[0], head_count, head_size)

    def one_block(query_block):
        query_heads = query_block.reshape(span, head_count, head_size)
        scores = (
            jnp.einsum("qhd,khd->hqk", query_heads, key_heads, preferred_element_type=jnp.float32)
            * scale
        )
        scores = jnp.where(alive[None, None, :], scores, NEG_FILL)
        highest = jnp.max(scores, axis=-1, keepdims=True)
        weights = jnp.exp(scores - highest)
        totals = jnp.sum(weights, axis=-1)
        mixed = jnp.einsum(
            "hqk,khd->qhd",
            weights.astype(jnp.bfloat16),
            value_heads,
            preferred_element_type=jnp.float32,
        )
        mixed = mixed / jnp.transpose(totals)[:, :, None]
        return mixed.reshape(span, head_count * head_size).astype(jnp.bfloat16)

    outputs = lax.map(one_block, queries.reshape(blocks, span, queries.shape[1]))
    return outputs.reshape(total_rows, queries.shape[1])


def on_device(img_q, img_k, img_v, cond_rows, prompt_len, ref_count, assign):
    group = lax.axis_index("grp")
    shard = lax.axis_index("sp")
    groups = lax.axis_size("grp")
    shards = lax.axis_size("sp")
    width = img_q.shape[2]
    head_size = HD
    head_count = width // head_size
    image_rows = img_q.shape[1]
    text_rows = cond_rows.shape[1]
    order = jnp.arange(groups, dtype=jnp.int32)
    owner = jnp.sum(jnp.where(assign == group, order, 0))
    owner_prompt = jnp.sum(jnp.where(order == owner, prompt_len, 0))
    owner_ref = jnp.sum(jnp.where(order == owner, ref_count, 0))
    text_total = text_rows * shards
    ref_slots = text_total - text_total // 2
    pieces = lax.all_gather(cond_rows, "grp", axis=0, tiled=True)
    matched = assign == group
    picked = jnp.sum(jnp.where(matched[:, None, None], pieces, jnp.zeros_like(pieces)), axis=0)
    text_q = picked[:, :width]
    text_k = picked[:, width : 2 * width]
    text_v = picked[:, 2 * width :]
    local_slots = shard * text_rows + jnp.arange(text_rows, dtype=jnp.int32)
    local_alive = slot_alive(local_slots, owner_ref, owner_prompt, ref_slots)
    image_q = img_q[0]
    image_k = img_k[0]
    image_v = img_v[0]
    per_device = -(-head_count // shards)
    extra = (per_device * shards - head_count) * head_size

    def widen(matrix):
        return jnp.pad(matrix, ((0, 0), (0, extra)))

    head_q, head_k, head_v = (
        lax.all_to_all(
            widen(jnp.concatenate([image_q, text_q], axis=0)),
            "sp",
            split_axis=1,
            concat_axis=0,
            tiled=True,
        ),
        lax.all_to_all(
            widen(jnp.concatenate([image_k, text_k], axis=0)),
            "sp",
            split_axis=1,
            concat_axis=0,
            tiled=True,
        ),
        lax.all_to_all(
            widen(jnp.concatenate([image_v, text_v], axis=0)),
            "sp",
            split_axis=1,
            concat_axis=0,
            tiled=True,
        ),
    )
    all_slots = jnp.arange(shards * text_rows, dtype=jnp.int32).reshape(shards, text_rows)
    key_alive = jnp.concatenate(
        [
            jnp.ones((shards, image_rows), dtype=bool),
            slot_alive(all_slots, owner_ref, owner_prompt, ref_slots),
        ],
        axis=1,
    ).reshape(-1)
    attended = block_attention(head_q, head_k, head_v, key_alive, per_device, head_size)
    returned = lax.all_to_all(attended, "sp", split_axis=0, concat_axis=1, tiled=True)
    mixed = returned[:, :width]
    image_out = mixed[:image_rows]
    text_out = jnp.where(
        local_alive[:, None], mixed[image_rows:], jnp.zeros_like(mixed[image_rows:])
    )
    return (image_out[None], text_out[None])


def solution(mesh):
    in_specs = (
        P("grp", "sp", None),
        P("grp", "sp", None),
        P("grp", "sp", None),
        P("grp", "sp", None),
        P(),
        P(),
        P(),
    )
    out_specs = (P("grp", "sp", None), P("grp", "sp", None))
    return jax.shard_map(
        on_device, mesh=mesh, in_specs=in_specs, out_specs=out_specs, check_vma=False
    )
```

profile of v0, /device:TPU:32, one launch (start us, length us, event | category | flops | bytes accessed | tf_op | source)
XLA Modules:
  0.0 229.4 jit_solution(3107240790678338064)
XLA Ops:
  7.9 1.3 select_reduce_fusion.1
  9.2 39.9 %all-gather.2.cloned.1.call-done = bf16[16,8,9216]{2,1,0:T(8,128)(2,1)} async-done(((bf16[1,8,9216]{2,1,0:T(8,128)(2,1)}), bf16[16,8,9216]{2,1,0:T(8,128)(2,1)}) %all-gather.2.cloned.1.call-update) | async-done | bytes 2359312 | tf_op jit(solution)/shard_map/all_gather | solution.py:67
  49.1 2.2 select_reduce_fusion
  51.4 1.1 copy.45
  52.5 8.8 %all-to-all-start.2 = ((bf16[136,16,256]{2,0,1:T(8,128)(2,1)}), bf16[136,16,256]{2,0,1:T(8,128)(2,1)S(1)}, u32[]{:S(2)}, u32[]{:S(2)}) async-start(bf16[136,16,256]{2,0,1:T(8,128)(2,1)} %bitcast.34), calls=%async_computation.2 | async-start | bytes 2228224 | tf_op jit(solution)/shard_map/all_to_all | solution.py:99
  61.4 1.3 fusion.25
  62.7 1.1 copy.46
  63.7 25.3 %all-to-all-done.2 = bf16[136,16,256]{2,0,1:T(8,128)(2,1)S(1)} async-done(((bf16[136,16,256]{2,0,1:T(8,128)(2,1)}), bf16[136,16,256]{2,0,1:T(8,128)(2,1)S(1)}, u32[]{:S(2)}, u32[]{:S(2)}) %all-to-all-start.2) | async-done | bytes 1114144 | tf_op jit(solution)/shard_map/all_to_all | solution.py:99
  89.0 7.1 %all-to-all-start.1 = ((bf16[136,16,256]{2,0,1:T(8,128)(2,1)}), bf16[136,16,256]{2,0,1:T(8,128)(2,1)S(1)}, u32[]{:S(2)}, u32[]{:S(2)}) async-start(bf16[136,16,256]{2,0,1:T(8,128)(2,1)} %bitcast.54), calls=%async_computation.1 | async-start | bytes 2228224 | tf_op jit(solution)/shard_map/all_to_all | solution.py:92
  96.2 1.1 copy.47
  97.2 27.4 %all-to-all-done.1 = bf16[136,16,256]{2,0,1:T(8,128)(2,1)S(1)} async-done(((bf16[136,16,256]{2,0,1:T(8,128)(2,1)}), bf16[136,16,256]{2,0,1:T(8,128)(2,1)S(1)}, u32[]{:S(2)}, u32[]{:S(2)}) %all-to-all-start.1) | async-done | bytes 1114144 | tf_op jit(solution)/shard_map/all_to_all | solution.py:92
  125.6 5.8 %all-to-all-start = ((bf16[136,16,256]{2,0,1:T(8,128)(2,1)}), bf16[136,16,256]{2,0,1:T(8,128)(2,1)S(1)}, u32[]{:S(2)}, u32[]{:S(2)}) async-start(bf16[136,16,256]{2,0,1:T(8,128)(2,1)} %bitcast.36), calls=%async_computation | async-start | bytes 2228224 | tf_op jit(solution)/shard_map/all_to_all | solution.py:85
  131.4 1.3 fusion.32
  132.8 1.2 fusion.31
  134.7 1.1 copy.32
  136.7 20.3 %all-to-all-done = bf16[136,16,256]{2,0,1:T(8,128)(2,1)S(1)} async-done(((bf16[136,16,256]{2,0,1:T(8,128)(2,1)}), bf16[136,16,256]{2,0,1:T(8,128)(2,1)S(1)}, u32[]{:S(2)}, u32[]{:S(2)}) %all-to-all-start) | async-done | bytes 1114144 | tf_op jit(solution)/shard_map/all_to_all | solution.py:85
  157.0 29.2 %while.11 = (s32[]{:T(128)}, bf16[4,544,256]{2,1,0:T(8,128)(2,1)}, pred[16,136]{1,0:T(8,128)(4,1)}, bf16[4,544,256]{2,1,0:T(8,128)(2,1)S(1)}, bf16[2176,2,128]{2...) while((s32[]{:T(128)}, bf16[4,544,256]{2,1,0:T(8,128)(2,1)}, ...), condition=%wide.wide.region_7.8_spmd, body=%wide.wide.region_4.7_spmd.sunk | while | flops 1238472576 | bytes 38465280 | solution.py:47
  157.1 1.8 fusion.52
  158.9 2.0 fusion.53
  161.0 2.2 fusion.54
  164.4 1.8 fusion.52
  166.3 2.0 fusion.53
  168.3 2.2 fusion.54
  171.7 1.8 fusion.52
  173.6 2.0 fusion.53
  175.6 2.2 fusion.54
  179.0 1.8 fusion.52
  180.9 2.0 fusion.53
  182.9 2.2 fusion.54
  186.2 8.3 %all-to-all-start.3 = ((bf16[16,136,256]{2,1,0:T(8,128)(2,1)}), bf16[16,136,256]{2,1,0:T(8,128)(2,1)S(1)}, u32[]{:S(2)}, u32[]{:S(2)}) async-start(bf16[16,136,256]{2,1,0:T(8,128)(2,1)} %bitcast.59), calls=%async_computation.3 | async-start | bytes 2228224 | tf_op jit(solution)/shard_map/all_to_all | solution.py:116
  194.5 1.2 compare_select_fusion
  195.8 25.0 %all-to-all-done.3 = bf16[16,136,256]{2,1,0:T(8,128)(2,1)S(1)} async-done(((bf16[16,136,256]{2,1,0:T(8,128)(2,1)}), bf16[16,136,256]{2,1,0:T(8,128)(2,1)S(1)}, u32[]{:S(2)}, u32[]{:S(2)}) %all-to-all-start.3) | async-done | bytes 1114144 | tf_op jit(solution)/shard_map/all_to_all | solution.py:116
  (55 shorter events, 10.0 us)
Async XLA Ops:
  7.2 42.0 %all-gather.2.cloned.1.call-start = ((), (), s32[]{:S(2)}) async-start(), calls=%async_computation.4 | async-start | bytes 2506752 | tf_op jit(solution)/shard_map/all_gather | solution.py:67
  49.1 2.2 copy-start.3
  52.5 8.9 %copy-start.4 = (bf16[1,128,3072]{2,1,0:T(8,128)(2,1)S(1)}, bf16[1,128,3072]{2,1,0:T(8,128)(2,1)}, u32[]{:S(2)}) copy-start(bf16[1,128,3072]{2,1,0:T(8,128)(2,1)} %param.9) | copy-start | bytes 2359300
  52.5 36.5 %all-to-all-start.2 = ((bf16[136,16,256]{2,0,1:T(8,128)(2,1)}), bf16[136,16,256]{2,0,1:T(8,128)(2,1)S(1)}, u32[]{:S(2)}, u32[]{:S(2)}) async-start(bf16[136,16,256]{2,0,1:T(8,128)(2,1)} %bitcast.34), calls=%async_computation.2 | async-start | bytes 2228224 | tf_op jit(solution)/shard_map/all_to_all | solution.py:99
  89.0 35.6 %all-to-all-start.1 = ((bf16[136,16,256]{2,0,1:T(8,128)(2,1)}), bf16[136,16,256]{2,0,1:T(8,128)(2,1)S(1)}, u32[]{:S(2)}, u32[]{:S(2)}) async-start(bf16[136,16,256]{2,0,1:T(8,128)(2,1)} %bitcast.54), calls=%async_computation.1 | async-start | bytes 2228224 | tf_op jit(solution)/shard_map/all_to_all | solution.py:92
  124.6 1.0 copy-start
  124.6 6.8 %copy-start.6 = (s32[16]{0:T(128)S(1)}, s32[16]{0:T(128)}, u32[]{:S(2)}) copy-start(s32[16]{0:T(128)} %param.14) | copy-start | bytes 196
  124.6 6.8 %copy-start.7 = (s32[16]{0:T(128)S(1)}, s32[16]{0:T(128)}, u32[]{:S(2)}) copy-start(s32[16]{0:T(128)} %param.13) | copy-start | bytes 196
  125.6 31.4 %all-to-all-start = ((bf16[136,16,256]{2,0,1:T(8,128)(2,1)}), bf16[136,16,256]{2,0,1:T(8,128)(2,1)S(1)}, u32[]{:S(2)}, u32[]{:S(2)}) async-start(bf16[136,16,256]{2,0,1:T(8,128)(2,1)} %bitcast.36), calls=%async_computation | async-start | bytes 2228224 | tf_op jit(solution)/shard_map/all_to_all | solution.py:85
  134.1 0.6 copy-start.5
  134.7 1.6 copy-start.1
  158.9 2.0 copy-start.2
  166.2 2.0 copy-start.2
  173.5 2.0 copy-start.2
  180.9 2.0 copy-start.2
  186.2 34.5 %all-to-all-start.3 = ((bf16[16,136,256]{2,1,0:T(8,128)(2,1)}), bf16[16,136,256]{2,1,0:T(8,128)(2,1)S(1)}, u32[]{:S(2)}, u32[]{:S(2)}) async-start(bf16[16,136,256]{2,1,0:T(8,128)(2,1)} %bitcast.59), calls=%async_computation.3 | async-start | bytes 2228224 | tf_op jit(solution)/shard_map/all_to_all | solution.py:116
Sparse Core Ops, SparseCore 0:
  9.8 39.2 all-gather.1
where the time goes:
time: 233 us; the launch traced here: 229 us
  waiting for transfers between devices  139 us (60%)
  starting transfers between devices  30.1 us (13%)
  other arithmetic  17.4 us (7%)
  matrix products  16.1 us (7%)
  between operations  14.2 us (6%)
  local copies, waits for them, and re-layouts  12.9 us (6%)
    all_gather x1, waiting for transfers between devices, on_device(): pieces = lax.all_gather(cond_rows, 'grp', axis=0, tiled=True)  39.9 us
    all_to_all x1, waiting for transfers between devices, on_device(): lax.all_to_all(widen(jnp.concatenate([image_k, text_k], axis=0)), 'sp', s...  27.4 us
    all_to_all x1, waiting for transfers between devices, on_device(): lax.all_to_all(widen(jnp.concatenate([image_v, text_v], axis=0)), 'sp', s...  25.3 us
    all_to_all x1, waiting for transfers between devices, on_device(): lax.all_to_all(attended, 'sp', split_axis=0, concat_axis=1, tiled=True)  25 us
    all_to_all x1, waiting for transfers between devices, on_device(): lax.all_to_all(widen(jnp.concatenate([image_q, text_q], axis=0)), 'sp', s...  20.3 us
    all_to_all x1, starting transfers between devices, on_device(): lax.all_to_all(widen(jnp.concatenate([image_v, text_v], axis=0)), 'sp', s...  8.84 us
    dot_general x4, matrix products, one_block(): jnp.einsum('hqk,khd->qhd', weights.astype(jnp.bfloat16), value_heads, pre...  8.81 us
    all_to_all x1, starting transfers between devices, on_device(): lax.all_to_all(attended, 'sp', split_axis=0, concat_axis=1, tiled=True)  8.29 us
  transfers between devices with their start and end apart: 5, of which 5 were waited for; matrix products, arithmetic and copies ran while one was open for 5% of the time, Pallas kernels for 0%

commit v1 on v0

v1 whole, which is shorter than its diff:
```python
import functools
import math

import jax
import jax.numpy as jnp
from jax import lax
from jax.experimental import pallas as pl
from jax.experimental.pallas import tpu as pltpu
from jax.sharding import PartitionSpec as P

HD = 128
NEG_FILL = -1e30
VMEM_LIMIT = 48 * 1024 * 1024


def call(body, out_shape, in_specs, out_specs, scratch_shapes=()):
    return pl.pallas_call(
        body,
        out_shape=out_shape,
        in_specs=in_specs,
        out_specs=out_specs,
        scratch_shapes=list(scratch_shapes),
        compiler_params=pltpu.CompilerParams(vmem_limit_bytes=VMEM_LIMIT),
    )


VMEM = pl.BlockSpec(memory_space=pltpu.VMEM)
SMEM = pl.BlockSpec(memory_space=pltpu.SMEM)


class Plan:
    def __init__(self, shards, rows, text_rows, width):
        self.shards = shards
        self.rows = rows
        self.half = rows // 2
        self.text_rows = text_rows
        self.width = width

    def side(self, device):
        return (device >> 2) & 1

    def shared(self, device):
        return self.shards + ((device >> 3) << 2) + (device & 3)


def head(column):
    return slice(column * HD, (column + 1) * HD)


def pack_first(plan, q, k, v, out):
    rows, half = plan.rows, plan.half
    for device in range(plan.shards):
        side, shared = plan.side(device), plan.shared(device)
        mine = slice(side * half, (side + 1) * half)
        out[device, 0:rows, :] = q[:, head(device)]
        out[device, rows : rows + half, :] = q[mine, head(shared)]
        out[device, rows + half : 2 * rows, :] = k[mine, head(shared)]
        out[device, 2 * rows : 2 * rows + half, :] = v[mine, head(shared)]


def pack_second(plan, k, v, text, out):
    rows = plan.rows
    heads = plan.width // HD
    wide = text[...].astype(jnp.float32)
    for device in range(plan.shards):
        out[device, 0:rows, :] = k[:, head(device)]
        out[device, rows : 2 * rows, :] = v[:, head(device)]
        pieces = [wide[:, head(part * heads + own)] for own in (device, plan.shared(device)) for part in range(3)]
        out[device, 2 * rows :, :] = jnp.concatenate(pieces, axis=0).astype(out.dtype)


def attend(queries, keys, values, alive, image_keys):
    factor = math.log2(math.e) / math.sqrt(HD)
    dims = (((1,), (1,)), ((), ()))
    image = lax.dot_general(queries, keys[:image_keys], dims, preferred_element_type=jnp.float32)
    text = lax.dot_general(queries, keys[image_keys:], dims, preferred_element_type=jnp.float32)
    text = jnp.where(alive, text, NEG_FILL)
    top = jnp.maximum(jnp.max(image, axis=1, keepdims=True), jnp.max(text, axis=1, keepdims=True))
    image = jnp.exp2((image - top) * factor).astype(jnp.bfloat16)
    text = jnp.exp2((text - top) * factor).astype(jnp.bfloat16)
    mixed = jnp.dot(image, values[:image_keys], preferred_element_type=jnp.float32)
    mixed = mixed + jnp.dot(text, values[image_keys:], preferred_element_type=jnp.float32)
    return (mixed[:, :HD] / mixed[:, HD:]).astype(jnp.bfloat16)


def owner_counts(group, assign, prompt_len, ref_count, groups):
    prompt, ref = prompt_len[0], ref_count[0]
    for request in range(1, groups):
        here = assign[request] == group
        prompt = jnp.where(here, prompt_len[request], prompt)
        ref = jnp.where(here, ref_count[request], ref)
    return prompt, ref


def attention(plan, groups, place, assign, prompt_len, ref_count, first, second, swapped, out, k_own, v_own, k_shared, v_shared, texts):
    rows, half, shards, text_rows = plan.rows, plan.half, plan.shards, plan.text_rows
    images = shards * rows
    slots = shards * text_rows
    prompt, ref = owner_counts(place[0], assign, prompt_len, ref_count, groups)
    ref_slots = slots - slots // 2
    slot = lax.broadcasted_iota(jnp.int32, (1, slots), 1)
    alive = slot < jnp.where(slot < ref_slots, ref, ref_slots + prompt)

    for values in (v_own, v_shared):
        values[:, HD:] = jnp.ones((images + slots, HD), jnp.bfloat16)
    for source in range(shards):
        at = source * rows
        k_own[at : at + rows, :] = second[source, 0:rows, :]
        v_own[at : at + rows, :HD] = second[source, rows : 2 * rows, :]
        mid = at + half
        k_shared[at:mid, :] = first[source, rows + half : 2 * rows, :]
        v_shared[at:mid, :HD] = first[source, 2 * rows : 2 * rows + half, :]
        k_shared[mid : at + rows, :] = swapped[source, 0:half, :]
        v_shared[mid : at + rows, :HD] = swapped[source, half : 2 * half, :]
    for source in range(0, shards, 2):
        one = second[source, 2 * rows :, :].astype(jnp.float32)
        two = second[source + 1, 2 * rows :, :].astype(jnp.float32)
        at = source * text_rows
        for part in range(6):
            cut = slice(part * text_rows, (part + 1) * text_rows)
            both = jnp.concatenate([one[cut], two[cut]], axis=0).astype(jnp.bfloat16)
            place_at = slice(at, at + 2 * text_rows)
            into = slice(images + at, images + at + 2 * text_rows)
            if part == 0:
                texts[0, place_at, :] = both
            elif part == 1:
                k_own[into, :] = both
            elif part == 2:
                v_own[into, :HD] = both
            elif part == 3:
                texts[1, place_at, :] = both
            elif part == 4:
                k_shared[into, :] = both
            else:
                v_shared[into, :HD] = both

    def own_block(step, carry):
        source = step * 2
        queries = first[pl.ds(source, 2), 0:rows, :].reshape(2 * rows, HD)
        mixed = attend(queries, k_own, v_own, alive, images)
        out[pl.ds(source, 2), 0:rows, :] = mixed.reshape(2, rows, HD)
        return carry

    def shared_block(step, carry):
        source = step * 4
        queries = first[pl.ds(source, 4), rows : rows + half, :].reshape(4 * half, HD)
        mixed = attend(queries, k_shared, v_shared, alive, images)
        out[pl.ds(source, 4), rows : rows + half, :] = mixed.reshape(4, half, HD)
        return carry

    lax.fori_loop(0, shards // 2, own_block, 0, unroll=2)
    lax.fori_loop(0, shards // 4, shared_block, 0, unroll=2)
    own_text = attend(texts[0], k_own, v_own, alive, images).astype(jnp.float32)
    shared_text = attend(texts[1], k_shared, v_shared, alive, images).astype(jnp.float32)
    for source in range(shards):
        cut = slice(source * text_rows, (source + 1) * text_rows)
        out[source, rows + half :, :] = jnp.concatenate([own_text[cut], shared_text[cut]], axis=0).astype(jnp.bfloat16)


def unpack(plan, groups, place, assign, prompt_len, ref_count, returned, image_out, text_out):
    rows, half, shards, text_rows = plan.rows, plan.half, plan.shards, plan.text_rows
    slots = shards * text_rows
    prompt, ref = owner_counts(place[0], assign, prompt_len, ref_count, groups)
    ref_slots = slots - slots // 2
    slot = place[1] * text_rows + lax.broadcasted_iota(jnp.int32, (text_rows, 1), 0)
    alive = slot < jnp.where(slot < ref_slots, ref, ref_slots + prompt)
    for device in range(shards):
        side, shared = plan.side(device), plan.shared(device)
        image_out[:, head(device)] = returned[device, 0:rows, :]
        image_out[side * half : (side + 1) * half, head(shared)] = returned[device, rows : rows + half, :]
        text = returned[device, rows + half :, :].astype(jnp.float32)
        text_out[:, head(device)] = jnp.where(alive, text[:text_rows], 0.0).astype(text_out.dtype)
        if side == 0:
            text_out[:, head(shared)] = jnp.where(alive, text[text_rows:], 0.0).astype(text_out.dtype)


def route(cond, group, assign, groups):
    order = jnp.arange(groups, dtype=jnp.int32)

    def exchange(data, bit):
        return lax.ppermute(data, "grp", [(i, i ^ bit) for i in range(groups)])

    def target(source):
        return jnp.sum(jnp.where(order == source, assign, 0))

    held = [cond, exchange(cond, 8)]
    other = exchange(jnp.stack(held), 1)
    held = held + [other[0], other[1]]
    targets = [target(group ^ bits) for bits in (0, 8, 1, 9)]

    def bound_for(place):
        total = jnp.zeros_like(cond)
        for packet, aim in zip(held, targets):
            total = jnp.where(aim == place, packet, total)
        return total

    came = exchange(jnp.stack([bound_for(group ^ 2), bound_for(group ^ 6)]), 2)
    mine = bound_for(group) + came[0]
    across = bound_for(group ^ 4) + came[1]
    return mine + exchange(across, 4)


def on_device(img_q, img_k, img_v, cond_rows, prompt_len, ref_count, assign):
    group = lax.axis_index("grp")
    shard = lax.axis_index("sp")
    groups = lax.axis_size("grp")
    shards = lax.axis_size("sp")
    _, rows, width = img_q.shape
    text_rows = cond_rows.shape[1]
    half = rows // 2
    plan = Plan(shards, rows, text_rows, width)
    place = jnp.stack([group, shard]).astype(jnp.int32)
    dtype = img_q.dtype

    def across(data):
        return lax.all_to_all(data, "sp", split_axis=0, concat_axis=0, tiled=True)

    text = route(cond_rows[0], group, assign, groups)
    first = call(
        functools.partial(pack_first, plan),
        jax.ShapeDtypeStruct((shards, 2 * rows + half, HD), dtype),
        [VMEM] * 3,
        VMEM,
    )(img_q[0], img_k[0], img_v[0])
    first = across(first)
    second = call(
        functools.partial(pack_second, plan),
        jax.ShapeDtypeStruct((shards, 2 * rows + 6 * text_rows, HD), dtype),
        [VMEM] * 3,
        VMEM,
    )(img_k[0], img_v[0], text)
    second = across(second)
    swapped = lax.ppermute(first[:, rows + half :, :], "sp", [(i, i ^ 4) for i in range(shards)])
    total = shards * (rows + text_rows)
    mixed = call(
        functools.partial(attention, plan, groups),
        jax.ShapeDtypeStruct((shards, rows + half + 2 * text_rows, HD), dtype),
        [SMEM] * 4 + [VMEM] * 3,
        VMEM,
        [
            pltpu.VMEM((total, HD), dtype),
            pltpu.VMEM((total, 2 * HD), dtype),
            pltpu.VMEM((total, HD), dtype),
            pltpu.VMEM((total, 2 * HD), dtype),
            pltpu.VMEM((2, shards * text_rows, HD), dtype),
        ],
    )(place, assign, prompt_len, ref_count, first, second, swapped)
    returned = across(mixed)
    image_out, text_out = call(
        functools.partial(unpack, plan, groups),
        (
            jax.ShapeDtypeStruct((rows, width), dtype),
            jax.ShapeDtypeStruct((text_rows, width), dtype),
        ),
        [SMEM] * 4 + [VMEM],
        (VMEM, VMEM),
    )(place, assign, prompt_len, ref_count, returned)
    return (image_out[None], text_out[None])


def solution(mesh):
    spec = P("grp", "sp", None)
    return jax.shard_map(
        on_device,
        mesh=mesh,
        in_specs=(spec, spec, spec, spec, P(), P(), P()),
        out_specs=(spec, spec),
        check_vma=False,
    )
```

time: 233 us -> 145 us (0.62); the launches traced: 229 us -> 144 us
  waiting for transfers between devices: 139 us -> 58.7 us
  blocking collectives: 0 us -> 27.9 us
  matrix products: 16.1 us -> 0 us
  Pallas kernels: 0 us -> 16 us
  local copies, waits for them, and re-layouts: 12.9 us -> 1.99 us
  other arithmetic: 17.4 us -> 6.75 us
  starting transfers between devices: 30.1 us -> 22.2 us
  between operations: 14.2 us -> 10.7 us
    all_to_all x4 -> x2, waiting for transfers between devices: 97.9 us -> 32.5 us  [across(): return lax.all_to_all(data, 'sp', split_axis=0, concat_axis=0, tiled=True)]
    all_gather x1 -> x0, waiting for transfers between devices: 39.9 us -> none  [on_device(): pieces = lax.all_gather(cond_rows, 'grp', axis=0, tiled=True)]
    all_to_all x0 -> x1, blocking collectives: none -> 27.9 us  [across(): return lax.all_to_all(data, 'sp', split_axis=0, concat_axis=0, tiled=True)]
    ppermute x0 -> x5, waiting for transfers between devices: none -> 26.2 us  [the longest x1 20 us: on_device(): lax.ppermute(first[:, rows + half:, :], 'sp', [(i, i ^ 4) for i in range(...]
    dot_general x8 -> x0, matrix products: 16.1 us -> none  [the longest x4 8.81 us: one_block(): jnp.einsum('hqk,khd->qhd', weights.astype(jnp.bfloat16), value_heads, pre...]
    pallas_call x0 -> x4, Pallas kernels: none -> 16 us  [the longest x1 11.8 us: on_device(): call(functools.partial(attention, plan, groups), jax.ShapeDtypeStruct((sh...]
    all_to_all x4 -> x2, starting transfers between devices: 30 us -> 14.1 us  [across(): return lax.all_to_all(data, 'sp', split_axis=0, concat_axis=0, tiled=True)]
    reduce_sum x7 -> x1, other arithmetic: 12.8 us -> 1.4 us  [target(): return jnp.sum(jnp.where(order == source, assign, 0))]
  transfers between devices with their start and end apart: 5 -> 7, of which waited for: 5 -> 5; matrix products, arithmetic and copies ran while one was open for 5% -> 3% of each run, Pallas kernels for 0% -> 2%
where the time goes in v1:
time: 145 us; the launch traced here: 144 us
  waiting for transfers between devices  58.7 us (40%)
  blocking collectives  27.9 us (19%)
  starting transfers between devices  22.2 us (15%)
  Pallas kernels  16 us (11%)
  between operations  10.7 us (7%)
  other arithmetic  6.75 us (5%)
  local copies, waits for them, and re-layouts  1.99 us (1%)
    all_to_all x2, waiting for transfers between devices, across(): return lax.all_to_all(data, 'sp', split_axis=0, concat_axis=0, tiled=True)  32.5 us
    all_to_all x1, blocking collectives, across(): return lax.all_to_all(data, 'sp', split_axis=0, concat_axis=0, tiled=True)  27.9 us
    ppermute x1, waiting for transfers between devices, on_device(): lax.ppermute(first[:, rows + half:, :], 'sp', [(i, i ^ 4) for i in range(...  20 us
    all_to_all x2, starting transfers between devices, across(): return lax.all_to_all(data, 'sp', split_axis=0, concat_axis=0, tiled=True)  14.1 us
    pallas_call x1, Pallas kernels, on_device(): call(functools.partial(attention, plan, groups), jax.ShapeDtypeStruct((sh...  11.8 us
    ppermute x4, starting transfers between devices, exchange(): return lax.ppermute(data, 'grp', [(i, i ^ bit) for i in range(groups)])  6.25 us
    ppermute x4, waiting for transfers between devices, exchange(): return lax.ppermute(data, 'grp', [(i, i ^ bit) for i in range(groups)])  6.23 us
  transfers between devices with their start and end apart: 7, of which 5 were waited for; matrix products, arithmetic and copies ran while one was open for 3% of the time, Pallas kernels for 2%

profile of v1, /device:TPU:32, one launch (start us, length us, event | category | flops | bytes accessed | tf_op | source)
XLA Modules:
  0.0 144.2 jit_solution(3896583580499263669)
XLA Ops:
  0.6 0.0 copy-start.1
  0.6 0.0 copy-start
  0.6 1.9 %collective-permute-start = (bf16[8,9216]{1,0:T(8,128)(2,1)}, bf16[8,9216]{1,0:T(8,128)(2,1)S(1)}, u32[]{:S(2)}, u32[]{:S(2)}) collective-permute-start(bf16[8,9216]{1,0:T(8,128)(2,1)} %bitcast.52), channel_id=1, source_target_pairs={{0,128},{16,144},{32,160},{48,176},{64,192},{80,208},{96,224},{112... | collective-permute-start | bytes 442376 | tf_op jit(solution)/shard_map/ppermute | solution.py:181
  2.6 4.0 %collective-permute-done = bf16[8,9216]{1,0:T(8,128)(2,1)S(1)} collective-permute-done((bf16[8,9216]{1,0:T(8,128)(2,1)}, bf16[8,9216]{1,0:T(8,128)(2,1)S(1)}, u32[]{:S(2)}, u32[]{:S(2)}) %collective-permute-start) | collective-permute-done | bytes 147488 | tf_op jit(solution)/shard_map/ppermute | solution.py:181
  6.5 0.9 pad_maximum_fusion
  7.5 0.1 collective-permute-start.1
  7.6 1.4 fusion.3
  14.0 0.0 collective-permute-done.1
  14.0 1.0 select_bitcast_fusion.1
  14.9 0.7 pad_maximum_fusion.1
  15.7 1.5 %collective-permute-start.2 = (bf16[2,8,9216]{2,1,0:T(8,128)(2,1)}, bf16[2,8,9216]{2,1,0:T(8,128)(2,1)}, u32[]{:S(2)}, u32[]{:S(2)}) collective-permute-start(bf16[2,8,9216]{2,1,0:T(8,128)(2,1)} %pad_maximum_fusion.1), channel_id=1, source_target_pairs={{0,32},{16,48},{32,0},{48,16},{64,96},{80,112},{96,64},{112,80},{1... | collective-permute-start | bytes 884744 | tf_op jit(solution)/shard_map/ppermute | solution.py:181
  17.2 0.0 copy-done
  17.2 1.1 copy-done.2
  18.3 1.3 shard_map.86
  19.6 10.4 %all-to-all-start = ((bf16[16,320,128]{2,1,0:T(8,128)(2,1)}), bf16[16,320,128]{2,1,0:T(8,128)(2,1)S(1)}, u32[]{:S(2)}, u32[]{:S(2)}) async-start(bf16[16,320,128]{2,1,0:T(8,128)(2,1)} %shard_map.86), calls=%async_computation | async-start | bytes 2621440 | tf_op jit(solution)/shard_map/all_to_all | solution.py:216
  32.6 0.0 collective-permute-done.2
  32.6 0.0 copy-done.6
  32.6 1.6 %fusion = bf16[8,9216]{1,0:T(8,128)(2,1)} fusion(bf16[2,8,9216]{2,1,0:T(8,128)(2,1)} %collective-permute-done.2, bf16[8,9216]{1,0:T(8,128)(2,1)S(1)} %collective-permute-done, pred[]{:T(512)S(6)} %eq.95, pred[]{:T(512)S(6)} %eq.94, pred[]{:T(512)S(6)} %eq.93, pred[]{:T(512)S(6)} %eq.92, bf16[2,8,9216]{2,1,0:T(8,128)(2,1)S(1)} %collective-permute-done.1, ...), kind=kLoop, calls=%fused_computation.3 | loop fusion | flops 368640 | bytes 884740 | tf_op jit(solution)/shard_map/add | solution.py:199
  34.2 2.7 %collective-permute-start.3 = (bf16[8,9216]{1,0:T(8,128)(2,1)}, bf16[8,9216]{1,0:T(8,128)(2,1)}, u32[]{:S(2)}, u32[]{:S(2)}) collective-permute-start(bf16[8,9216]{1,0:T(8,128)(2,1)} %fusion), channel_id=1, source_target_pairs={{0,64},{16,80},{32,96},{48,112},{64,0},{80,16},{96,32},{112,48},{1... | collective-permute-start | bytes 442376 | tf_op jit(solution)/shard_map/ppermute | solution.py:181
  39.4 2.3 %collective-permute-done.3 = bf16[8,9216]{1,0:T(8,128)(2,1)} collective-permute-done((bf16[8,9216]{1,0:T(8,128)(2,1)}, bf16[8,9216]{1,0:T(8,128)(2,1)}, u32[]{:S(2)}, u32[]{:S(2)}) %collective-permute-start.3) | collective-permute-done | bytes 147488 | tf_op jit(solution)/shard_map/ppermute | solution.py:181
  41.7 1.0 fusion.2.text
  42.7 1.2 shard_map.87
  44.0 22.0 %all-to-all-done.first = bf16[16,320,128]{2,1,0:T(8,128)(2,1)S(1)} async-done(((bf16[16,320,128]{2,1,0:T(8,128)(2,1)}), bf16[16,320,128]{2,1,0:T(8,128)(2,1)S(1)}, u32[]{:S(2)}, u32[]{:S(2)}) %all-to-all-start) | async-done | bytes 1310752 | tf_op jit(solution)/shard_map/all_to_all | solution.py:216
  65.9 3.7 %all-to-all-start.1 = ((bf16[16,304,128]{2,1,0:T(8,128)(2,1)}), bf16[16,304,128]{2,1,0:T(8,128)(2,1)S(1)}, u32[]{:S(2)}, u32[]{:S(2)}) async-start(bf16[16,304,128]{2,1,0:T(8,128)(2,1)} %shard_map.87), calls=%async_computation.1 | async-start | bytes 2490368 | tf_op jit(solution)/shard_map/all_to_all | solution.py:216
  69.6 0.8 slice.24
  70.5 1.8 %collective-permute-start.4 = (bf16[16,128,128]{2,1,0:T(8,128)(2,1)}, bf16[16,128,128]{2,1,0:T(8,128)(2,1)S(1)}, u32[]{:S(2)}, u32[]{:S(2)}) collective-permute-start(bf16[16,128,128]{2,1,0:T(8,128)(2,1)} %slice.24), channel_id=1, source_target_pairs={{0,4},{1,5},{2,6},{3,7},{4,0},{5,1},{6,2},{7,3},{8,12},{9,13},{10,... | collective-permute-start | bytes 1572872 | tf_op jit(solution)/shard_map/ppermute | solution.py:233
  72.3 0.1 pad_add_fusion.place
  72.4 20.0 %collective-permute-done.4.swapped = bf16[16,128,128]{2,1,0:T(8,128)(2,1)S(1)} collective-permute-done((bf16[16,128,128]{2,1,0:T(8,128)(2,1)}, bf16[16,128,128]{2,1,0:T(8,128)(2,1)S(1)}, u32[]{:S(2)}, u32[]{:S(2)}) %collective-permute-start.4) | collective-permute-done | bytes 524320 | tf_op jit(solution)/shard_map/ppermute | solution.py:233
  92.4 10.5 %all-to-all-done.1.second = bf16[16,304,128]{2,1,0:T(8,128)(2,1)S(1)} async-done(((bf16[16,304,128]{2,1,0:T(8,128)(2,1)}), bf16[16,304,128]{2,1,0:T(8,128)(2,1)S(1)}, u32[]{:S(2)}, u32[]{:S(2)}) %all-to-all-start.1) | async-done | bytes 1245216 | tf_op jit(solution)/shard_map/all_to_all | solution.py:216
  102.9 11.8 %shard_map.88 = bf16[16,208,128]{2,1,0:T(8,128)(2,1)S(1)} custom-call(s32[2]{0:T(128)S(1)} %pad_add_fusion.place, s32[16]{0:T(128)S(1)} %copy-done.3, s32[16]{0:T(128)S(1)} %copy-done.4, s32[16]{0:T(128)S(1)} %copy-done.5, bf16[16,320,128]{2,1,0:T(8,128)(2,1)S(1)} %all-to-all-done.first, bf16[16,304,128]{2,1,0:T(8,128)(2,1)S(1)} %all-to-all-done.1.second, ...), custom_call_target="tpu_custom_call" | custom-call | tf_op jit(solution)/shard_map/pallas_call | solution.py:235
  114.7 27.9 %all_to_all.15.returned = bf16[16,208,128]{2,1,0:T(8,128)(2,1)S(1)} all-to-all(bf16[16,208,128]{2,1,0:T(8,128)(2,1)S(1)} %shard_map.88), channel_id=1, replica_groups=mesh['grp'=16,'sp'=16] {'sp'}, dimensions={0} | all-to-all | bytes 1703936 | tf_op jit(solution)/shard_map/all_to_all | solution.py:216
  142.5 1.6 %shard_map.89 = (bf16[128,3072]{1,0:T(8,128)(2,1)}, bf16[8,3072]{1,0:T(8,128)(2,1)}) custom-call(s32[2]{0:T(128)S(1)} %pad_add_fusion.place, s32[16]{0:T(128)S(1)} %copy-done.3, s32[16]{0:T(128)S(1)} %copy-done.4, s32[16]{0:T(128)S(1)} %copy-done.5, bf16[16,208,128]{2,1,0:T(8,128)(2,1)S(1)} %all_to_all.15.returned), custom_call_target="tpu_custom_call" | custom-call | tf_op jit(solution)/shard_map/pallas_call | solution.py:249
  (9 shorter events, 0.0 us)
Async XLA Ops:
  0.6 16.6 %copy-start.1 = (bf16[1,128,3072]{2,1,0:T(8,128)(2,1)S(1)}, bf16[1,128,3072]{2,1,0:T(8,128)(2,1)}, u32[]{:S(2)}) copy-start(bf16[1,128,3072]{2,1,0:T(8,128)(2,1)} %param.9) | copy-start | bytes 2359300
  0.6 16.5 %copy-start = (bf16[1,128,3072]{2,1,0:T(8,128)(2,1)S(1)}, bf16[1,128,3072]{2,1,0:T(8,128)(2,1)}, u32[]{:S(2)}) copy-start(bf16[1,128,3072]{2,1,0:T(8,128)(2,1)} %param.8) | copy-start | bytes 2359300
  0.6 5.9 %collective-permute-start = (bf16[8,9216]{1,0:T(8,128)(2,1)}, bf16[8,9216]{1,0:T(8,128)(2,1)S(1)}, u32[]{:S(2)}, u32[]{:S(2)}) collective-permute-start(bf16[8,9216]{1,0:T(8,128)(2,1)} %bitcast.52), channel_id=1, source_target_pairs={{0,128},{16,144},{32,160},{48,176},{64,192},{80,208},{96,224},{112... | collective-permute-start | bytes 442376 | tf_op jit(solution)/shard_map/ppermute | solution.py:181
  7.5 6.5 %collective-permute-start.1 = (bf16[2,8,9216]{2,1,0:T(8,128)(2,1)S(1)}, bf16[2,8,9216]{2,1,0:T(8,128)(2,1)S(1)}, u32[]{:S(2)}, u32[]{:S(2)}) collective-permute-start(bf16[2,8,9216]{2,1,0:T(8,128)(2,1)S(1)} %pad_maximum_fusion), channel_id=1, source_target_pairs={{0,16},{16,0},{32,48},{48,32},{64,80},{80,64},{96,112},{112,96},{1... | collective-permute-start | bytes 884744 | tf_op jit(solution)/shard_map/ppermute | solution.py:181
  15.7 16.9 %collective-permute-start.2 = (bf16[2,8,9216]{2,1,0:T(8,128)(2,1)}, bf16[2,8,9216]{2,1,0:T(8,128)(2,1)}, u32[]{:S(2)}, u32[]{:S(2)}) collective-permute-start(bf16[2,8,9216]{2,1,0:T(8,128)(2,1)} %pad_maximum_fusion.1), channel_id=1, source_target_pairs={{0,32},{16,48},{32,0},{48,16},{64,96},{80,112},{96,64},{112,80},{1... | collective-permute-start | bytes 884744 | tf_op jit(solution)/shard_map/ppermute | solution.py:181
  17.2 1.1 copy-start.2
  19.6 13.0 %copy-start.6 = (bf16[1,8,9216]{2,1,0:T(8,128)(2,1)S(1)}, bf16[1,8,9216]{2,1,0:T(8,128)(2,1)}, u32[]{:S(2)}) copy-start(bf16[1,8,9216]{2,1,0:T(8,128)(2,1)} %param.10) | copy-start | bytes 442372
  19.6 46.3 %all-to-all-start = ((bf16[16,320,128]{2,1,0:T(8,128)(2,1)}), bf16[16,320,128]{2,1,0:T(8,128)(2,1)S(1)}, u32[]{:S(2)}, u32[]{:S(2)}) async-start(bf16[16,320,128]{2,1,0:T(8,128)(2,1)} %shard_map.86), calls=%async_computation | async-start | bytes 2621440 | tf_op jit(solution)/shard_map/all_to_all | solution.py:216
  34.2 7.5 %collective-permute-start.3 = (bf16[8,9216]{1,0:T(8,128)(2,1)}, bf16[8,9216]{1,0:T(8,128)(2,1)}, u32[]{:S(2)}, u32[]{:S(2)}) collective-permute-start(bf16[8,9216]{1,0:T(8,128)(2,1)} %fusion), channel_id=1, source_target_pairs={{0,64},{16,80},{32,96},{48,112},{64,0},{80,16},{96,32},{112,48},{1... | collective-permute-start | bytes 442376 | tf_op jit(solution)/shard_map/ppermute | solution.py:181
  44.0 58.9 %copy-start.3 = (s32[16]{0:T(128)S(1)}, s32[16]{0:T(128)}, u32[]{:S(2)}) copy-start(s32[16]{0:T(128)} %assign.3) | copy-start | bytes 196
  44.0 58.9 %copy-start.4 = (s32[16]{0:T(128)S(1)}, s32[16]{0:T(128)}, u32[]{:S(2)}) copy-start(s32[16]{0:T(128)} %prompt_len.3) | copy-start | bytes 196
  44.0 58.9 %copy-start.5 = (s32[16]{0:T(128)S(1)}, s32[16]{0:T(128)}, u32[]{:S(2)}) copy-start(s32[16]{0:T(128)} %ref_count.3) | copy-start | bytes 196
  65.9 37.0 %all-to-all-start.1 = ((bf16[16,304,128]{2,1,0:T(8,128)(2,1)}), bf16[16,304,128]{2,1,0:T(8,128)(2,1)S(1)}, u32[]{:S(2)}, u32[]{:S(2)}) async-start(bf16[16,304,128]{2,1,0:T(8,128)(2,1)} %shard_map.87), calls=%async_computation.1 | async-start | bytes 2490368 | tf_op jit(solution)/shard_map/all_to_all | solution.py:216
  70.5 21.9 %collective-permute-start.4 = (bf16[16,128,128]{2,1,0:T(8,128)(2,1)}, bf16[16,128,128]{2,1,0:T(8,128)(2,1)S(1)}, u32[]{:S(2)}, u32[]{:S(2)}) collective-permute-start(bf16[16,128,128]{2,1,0:T(8,128)(2,1)} %slice.24), channel_id=1, source_target_pairs={{0,4},{1,5},{2,6},{3,7},{4,0},{5,1},{6,2},{7,3},{8,12},{9,13},{10,... | collective-permute-start | bytes 1572872 | tf_op jit(solution)/shard_map/ppermute | solution.py:233

commit v2 on v0

v2 whole, which is shorter than its diff:
```python
import functools
import math

import jax
import jax.numpy as jnp
from jax import lax
from jax.experimental import pallas as pl
from jax.experimental.pallas import tpu as pltpu
from jax.sharding import PartitionSpec as P

HD = 128
SIDE = 4
NEG_FILL = -1e30
FLOPS_S = 30000000000
KEY_SPAN = 512
FACTOR = math.log2(math.e) / math.sqrt(HD)
VMEM_LIMIT = 48 * 1024 * 1024
VMEM = pl.BlockSpec(memory_space=pltpu.VMEM)
SMEM = pl.BlockSpec(memory_space=pltpu.SMEM)
HBM = pl.BlockSpec(memory_space=pltpu.HBM)


def call(body, out_shape, in_specs, out_specs, scratch_shapes=(), grid=(), cost=None):
    return pl.pallas_call(
        body,
        grid=grid,
        cost_estimate=cost,
        out_shape=out_shape,
        in_specs=in_specs,
        out_specs=out_specs,
        scratch_shapes=list(scratch_shapes),
        compiler_params=pltpu.CompilerParams(vmem_limit_bytes=VMEM_LIMIT),
    )


class Plan:
    def __init__(self, groups, shards, rows, text_rows, width):
        self.groups = groups
        self.shards = shards
        self.rows = rows
        self.half = rows // 2
        self.text_rows = text_rows
        self.heads = width // HD
        self.slots = shards * text_rows
        self.images = shards * rows

    def side(self, device):
        return (device // SIDE) % 2

    def shared(self, device):
        return self.shards + (device // SIDE // 2) * SIDE + device % SIDE


def head(column):
    return slice(column * HD, (column + 1) * HD)


def head_at(column):
    return pl.ds(pl.multiple_of(column * HD, HD), HD)


def step_to(place, dy, dz):
    return lax.rem(place[1] + dy, SIDE), lax.rem(place[2] + dz, SIDE)


def step_from(place, dy, dz):
    y, z = step_to(place, SIDE - dy, SIDE - dz)
    return y * SIDE + z


def fetch(refs, columns, held, sems):
    copies = [pltpu.make_async_copy(ref.at[:, columns], held.at[part], sems.at[part]) for part, ref in enumerate(refs)]
    for copy in copies:
        copy.start()
    for copy in copies:
        copy.wait()


def pack_shared(plan, place, q, k, v, *rest):
    rows, first = plan.rows, plan.shards * HD
    outs, (held, sems) = rest[:SIDE], rest[SIDE:]
    fetch((q, k, v), slice(first, plan.heads * HD), held, sems)
    for dz in range(SIDE):
        z = lax.rem(place[2] + dz, SIDE)
        for pair in range(2):
            for part in range(3):
                outs[dz][pair, part * rows : (part + 1) * rows, :] = held[part, :, head_at(pair * SIDE + z)]


def pack_whole(plan, place, assign, q, k, v, h0, h2, h4, h6, early, out):
    rows = plan.rows
    owner = jnp.int32(0)
    for request in range(1, plan.groups):
        owner = jnp.where(assign[request] == place[0], request, owner)
    came = lax.rem(lax.div(lax.bitwise_xor(owner, place[0]), 2), 4)
    for device in range(plan.shards):
        for part, ref in enumerate((q, k, v)):
            out[device, part * rows : (part + 1) * rows, :] = ref[:, head(device)]
        pieces = []
        for own in (device, plan.shared(device)):
            for part in range(3):
                at = head(part * plan.heads + own)
                low = jnp.where(came == 0, h0[:, at].astype(jnp.float32), h2[:, at].astype(jnp.float32))
                high = jnp.where(came == 2, h4[:, at].astype(jnp.float32), h6[:, at].astype(jnp.float32))
                pieces.append(jnp.where(came < 2, low, high))
        out[device, 3 * rows :, :] = jnp.concatenate(pieces, axis=0).astype(jnp.bfloat16)


def choose(place, assign, h0, h8, h1, h9, *outs):
    group = place[0]
    for turn, out in zip((0, 2, 4, 6), outs):
        target = lax.bitwise_xor(group, turn)
        out[...] = h0[...]
        for bits, ref in ((1, h1), (8, h8), (9, h9)):

            @pl.when(assign[lax.bitwise_xor(group, bits)] == target)
            def _(ref=ref, out=out):
                out[...] = ref[...]


def regroup_shared(plan, place, *refs):
    rows, half = plan.rows, plan.half
    ins, outs = refs[:SIDE], refs[SIDE:]
    for dy in range(SIDE):
        y = lax.rem(place[1] + dy, SIDE)
        pair, side = lax.div(y, 2), lax.rem(y, 2)
        mine = pl.ds(pl.multiple_of(side * half, half), half)
        for dz in range(SIDE):
            outs[dy][dz, 0:half, :] = ins[dz][pair, mine, :]
            outs[dy][dz, half:, :] = ins[dz][pair, rows:, :]


def owner_counts(plan, place, assign, prompt_len, ref_count):
    prompt, ref = prompt_len[0], ref_count[0]
    for request in range(1, plan.groups):
        here = assign[request] == place[0]
        prompt = jnp.where(here, prompt_len[request], prompt)
        ref = jnp.where(here, ref_count[request], ref)
    return prompt, ref


def is_alive(plan, slot, counts):
    prompt, ref = counts
    ref_slots = plan.slots - plan.slots // 2
    return slot < jnp.where(slot < ref_slots, ref, ref_slots + prompt)


def scores(queries, keys):
    return lax.dot_general(queries, keys, (((1,), (1,)), ((), ())), preferred_element_type=jnp.float32)


def weights(score, top):
    return jnp.exp2((score - top) * FACTOR).astype(jnp.bfloat16)


def largest(score):
    return jnp.max(score, axis=1, keepdims=True)


def total(weight, values):
    return jnp.dot(weight, values, preferred_element_type=jnp.float32)


def attend(queries, pieces):
    mixed = top = None
    for keys, values, alive in pieces:
        score = scores(queries, keys)
        if alive is not None:
            score = jnp.where(alive, score, NEG_FILL)
        higher = largest(score)
        if top is not None:
            higher = jnp.maximum(top, higher)
        part = total(weights(score, higher), values)
        mixed = part if top is None else mixed * jnp.exp2((top - higher) * FACTOR) + part
        top = higher
    return (mixed[:, :HD] / mixed[:, HD:]).astype(jnp.bfloat16)


def attention(plan, place, assign, prompt_len, ref_count, came, p0, p1, p2, p3, out, keys, values, texts, text_values):
    rows, half, images, text_rows, slots = plan.rows, plan.half, plan.images, plan.text_rows, plan.slots
    alive = is_alive(plan, lax.broadcasted_iota(jnp.int32, (1, slots), 1), owner_counts(plan, place, assign, prompt_len, ref_count))
    parts = (p0, p1, p2, p3)
    for source in range(0, plan.shards, 2):
        pair = [came[source + i, 3 * rows :, :].astype(jnp.float32) for i in range(2)]
        at = source * text_rows
        for kind in range(6):
            cut = slice(kind * text_rows, (kind + 1) * text_rows)
            both = jnp.concatenate([one[cut] for one in pair], axis=0).astype(jnp.bfloat16)
            if kind in (2, 5):
                text_values[kind // 3, at : at + 2 * text_rows, :HD] = both
            else:
                texts[kind, at : at + 2 * text_rows, :] = both
    text_values[:, :, HD:] = jnp.ones((2, slots, HD), jnp.bfloat16)
    for source in range(plan.shards):
        at = slice(source * rows, (source + 1) * rows)
        keys[0, at, :] = came[source, rows : 2 * rows, :]
        values[0, at, :HD] = came[source, 2 * rows : 3 * rows, :]
        part, dz = parts[source // SIDE], source % SIDE
        keys[1, at, :] = part[dz, half : half + rows, :]
        values[1, at, :HD] = part[dz, half + rows :, :]
    values[:, :, HD:] = jnp.ones((2, images, HD), jnp.bfloat16)

    def mix(which, queries):
        cuts = [slice(at, at + KEY_SPAN) for at in range(0, images, KEY_SPAN)]
        pieces = [(keys[which, cut, :], values[which, cut, :], None) for cut in cuts]
        return attend(queries, pieces + [(texts[3 * which + 1], text_values[which], alive)])

    for source in range(0, plan.shards, 2):
        mixed = mix(0, came[source : source + 2, 0:rows, :].reshape(2 * rows, HD))
        out[source : source + 2, 0:rows, :] = mixed.reshape(2, rows, HD)
    for dy in range(SIDE):
        mixed = mix(1, parts[dy][:, 0:half, :].reshape(SIDE * half, HD))
        for dz in range(SIDE):
            out[step_from(place, dy, dz), rows : rows + half, :] = mixed[dz * half : (dz + 1) * half]
    own_text, other_text = (mix(which, texts[3 * which]).astype(jnp.float32) for which in range(2))
    for source in range(plan.shards):
        cut = slice(source * text_rows, (source + 1) * text_rows)
        out[source, rows + half :, :] = jnp.concatenate([own_text[cut], other_text[cut]], axis=0).astype(jnp.bfloat16)


def unpack(plan, place, assign, prompt_len, ref_count, returned, image_out, text_out):
    rows, half, text_rows = plan.rows, plan.half, plan.text_rows
    slot = (place[1] * SIDE + place[2]) * text_rows + lax.broadcasted_iota(jnp.int32, (text_rows, 1), 0)
    alive = is_alive(plan, slot, owner_counts(plan, place, assign, prompt_len, ref_count))
    for device in range(plan.shards):
        side, shared = plan.side(device), plan.shared(device)
        image_out[:, head(device)] = returned[device, 0:rows, :]
        image_out[side * half : (side + 1) * half, head(shared)] = returned[device, rows : rows + half, :]
        text = returned[device, rows + half :, :].astype(jnp.float32)
        text_out[:, head(device)] = jnp.where(alive, text[:text_rows], 0.0).astype(text_out.dtype)
        if side == 0:
            text_out[:, head(shared)] = jnp.where(alive, text[text_rows:], 0.0).astype(text_out.dtype)


def route(plan, place, assign, rows):
    def exchange(data, bits):
        return lax.ppermute(data, "grp", [(i, i ^ bits) for i in range(plan.groups)])

    held = [rows] + [exchange(rows, bits) for bits in (8, 1, 9)]
    shape = jax.ShapeDtypeStruct(rows.shape, rows.dtype)
    bound = call(choose, (shape,) * 4, [SMEM] * 2 + [VMEM] * 4, (VMEM,) * 4)(place, assign, *held)
    return [bound[0]] + [exchange(packet, bits) for packet, bits in zip(bound[1:], (2, 4, 6))]


def shift(data, dy, dz, shards):
    pairs = [(i, (i // SIDE + dy) % SIDE * SIDE + (i + dz) % SIDE) for i in range(shards)]
    return lax.ppermute(data, "sp", pairs)


def along_z(parts, shards):
    return [parts[0]] + [shift(parts[dz], 0, dz, shards) for dz in range(1, SIDE)]


def along_y(parts, shards):
    return [parts[0]] + [shift(parts[dy], dy, 0, shards) for dy in range(1, SIDE)]


def on_device(img_q, img_k, img_v, cond_rows, prompt_len, ref_count, assign):
    group = lax.axis_index("grp")
    shard = lax.axis_index("sp")
    groups = lax.axis_size("grp")
    shards = lax.axis_size("sp")
    _, rows, width = img_q.shape
    text_rows = cond_rows.shape[1]
    half = rows // 2
    plan = Plan(groups, shards, rows, text_rows, width)
    place = jnp.stack([group, shard // SIDE, shard % SIDE]).astype(jnp.int32)
    dtype = img_q.dtype

    def like(*shape, dtype=dtype):
        return jax.ShapeDtypeStruct(shape, dtype)

    images = (img_q[0], img_k[0], img_v[0])
    shared = width - shards * HD
    parts = call(
        functools.partial(pack_shared, plan),
        (like(2, 3 * rows, HD),) * SIDE,
        [SMEM] + [HBM] * 3,
        (VMEM,) * SIDE,
        [pltpu.VMEM((3, rows, shared), dtype), pltpu.SemaphoreType.DMA((3,))],
    )(place, *images)
    parts = along_z(parts, shards)
    early = parts[1]
    parts = call(
        functools.partial(regroup_shared, plan),
        (like(SIDE, half + 2 * rows, HD),) * SIDE,
        [SMEM] + [VMEM] * SIDE,
        (VMEM,) * SIDE,
        cost=pl.CostEstimate(flops=FLOPS_S, transcendentals=0, bytes_accessed=0),
    )(place, *parts)
    parts = along_y(parts, shards)

    texts = route(plan, place, assign, cond_rows[0])
    whole = call(
        functools.partial(pack_whole, plan),
        like(shards, 3 * rows + 6 * text_rows, HD),
        [SMEM] * 2 + [VMEM] * 7 + [pl.BlockSpec(memory_space=pl.ANY)],
        VMEM,
    )(place, assign, *images, *texts, early)
    whole = lax.all_to_all(whole, "sp", split_axis=0, concat_axis=0, tiled=True)

    lengths = (assign, prompt_len, ref_count)
    mixed = call(
        functools.partial(attention, plan),
        like(shards, rows + half + 2 * text_rows, HD),
        [SMEM] * 4 + [VMEM] * 5,
        VMEM,
        [
            pltpu.VMEM((2, plan.images, HD), dtype),
            pltpu.VMEM((2, plan.images, 2 * HD), dtype),
            pltpu.VMEM((6, plan.slots, HD), dtype),
            pltpu.VMEM((2, plan.slots, 2 * HD), dtype),
        ],
    )(place, *lengths, whole, *parts)
    returned = lax.all_to_all(mixed, "sp", split_axis=0, concat_axis=0, tiled=True)
    image_out, text_out = call(
        functools.partial(unpack, plan),
        (like(rows, width), like(text_rows, width)),
        [SMEM] * 4 + [VMEM],
        (VMEM, VMEM),
    )(place, *lengths, returned)
    return (image_out[None], text_out[None])


def solution(mesh):
    spec = P("grp", "sp", None)
    return jax.shard_map(
        on_device,
        mesh=mesh,
        in_specs=(spec, spec, spec, spec, P(), P(), P()),
        out_specs=(spec, spec),
        check_vma=False,
    )
```

time: 233 us -> 124 us (0.53); the launches traced: 229 us -> 123 us
  waiting for transfers between devices: 139 us -> 38.7 us
  blocking collectives: 0 us -> 30 us
  other arithmetic: 17.4 us -> 0.08 us
  Pallas kernels: 0 us -> 17.1 us
  matrix products: 16.1 us -> 0 us
  between operations: 14.2 us -> 0.76 us
  local copies, waits for them, and re-layouts: 12.9 us -> 3.43 us
  starting transfers between devices: 30.1 us -> 33.1 us
    all_to_all x4 -> x1, waiting for transfers between devices: 97.9 us -> 10.8 us  [on_device(): whole = lax.all_to_all(whole, 'sp', split_axis=0, concat_axis=0, tiled=True)]
    all_gather x1 -> x0, waiting for transfers between devices: 39.9 us -> none  [on_device(): pieces = lax.all_gather(cond_rows, 'grp', axis=0, tiled=True)]
    all_to_all x0 -> x1, blocking collectives: none -> 30 us  [on_device(): lax.all_to_all(mixed, 'sp', split_axis=0, concat_axis=0, tiled=True)]
    ppermute x0 -> x12, waiting for transfers between devices: none -> 28 us  [the longest x6 28 us: shift(): return lax.ppermute(data, 'sp', pairs)]
    ppermute x0 -> x12, starting transfers between devices: none -> 23.4 us  [the longest x6 16.4 us: shift(): return lax.ppermute(data, 'sp', pairs)]
    all_to_all x4 -> x1, starting transfers between devices: 30 us -> 9.64 us  [on_device(): whole = lax.all_to_all(whole, 'sp', split_axis=0, concat_axis=0, tiled=True)]
    pallas_call x0 -> x6, Pallas kernels: none -> 17.1 us  [the longest x1 11.2 us: on_device(): call(functools.partial(attention, plan), like(shards, rows + half + 2 * t...]
    dot_general x8 -> x0, matrix products: 16.1 us -> none  [the longest x4 8.81 us: one_block(): jnp.einsum('hqk,khd->qhd', weights.astype(jnp.bfloat16), value_heads, pre...]
  transfers between devices with their start and end apart: 5 -> 13, of which waited for: 5 -> 4; matrix products, arithmetic and copies ran while one was open for 5% -> 0% of each run, Pallas kernels for 0% -> 3%
where the time goes in v2:
time: 124 us; the launch traced here: 123 us
  waiting for transfers between devices  38.7 us (31%)
  starting transfers between devices  33.1 us (27%)
  blocking collectives  30 us (24%)
  Pallas kernels  17.1 us (14%)
  local copies, waits for them, and re-layouts  3.43 us (3%)
    all_to_all x1, blocking collectives, on_device(): lax.all_to_all(mixed, 'sp', split_axis=0, concat_axis=0, tiled=True)  30 us
    ppermute x6, waiting for transfers between devices, shift(): return lax.ppermute(data, 'sp', pairs)  28 us
    ppermute x6, starting transfers between devices, shift(): return lax.ppermute(data, 'sp', pairs)  16.4 us
    pallas_call x1, Pallas kernels, on_device(): call(functools.partial(attention, plan), like(shards, rows + half + 2 * t...  11.2 us
    all_to_all x1, waiting for transfers between devices, on_device(): whole = lax.all_to_all(whole, 'sp', split_axis=0, concat_axis=0, tiled=True)  10.8 us
    all_to_all x1, starting transfers between devices, on_device(): whole = lax.all_to_all(whole, 'sp', split_axis=0, concat_axis=0, tiled=True)  9.64 us
    ppermute x6, starting transfers between devices, exchange(): lax.ppermute(data, 'grp', [(i, i ^ bits) for i in range(plan.groups)])  7.01 us
    unnamed x18, local copies, waits for them, and re-layouts  3.43 us
  transfers between devices with their start and end apart: 13, of which 4 were waited for; matrix products, arithmetic and copies ran while one was open for 0% of the time, Pallas kernels for 3%

profile of v2, /device:TPU:32, one launch (start us, length us, event | category | flops | bytes accessed | tf_op | source)
XLA Modules:
  0.0 123.3 jit_solution(11256530306831194343)
XLA Ops:
  0.6 1.9 %collective-permute-start = (bf16[8,9216]{1,0:T(8,128)(2,1)}, bf16[8,9216]{1,0:T(8,128)(2,1)S(1)}, u32[]{:S(2)}, u32[]{:S(2)}) collective-permute-start(bf16[8,9216]{1,0:T(8,128)(2,1)} %bitcast.15), channel_id=1, source_target_pairs={{0,128},{16,144},{32,160},{48,176},{64,192},{80,208},{96,224},{112... | collective-permute-start | bytes 442376 | tf_op jit(solution)/shard_map/ppermute | solution.py:237
  2.6 0.3 collective-permute-start.2
  2.9 0.1 pad_add_fusion.place
  2.9 1.1 copy-done
  4.1 1.1 copy-done.2
  5.2 1.1 copy-done.4
  6.4 0.8 shard_map.87
  7.2 3.3 %collective-permute-start.6 = (bf16[2,384,128]{2,1,0:T(8,128)(2,1)S(1)}, bf16[2,384,128]{2,1,0:T(8,128)(2,1)S(1)}, u32[]{:S(2)}, u32[]{:S(2)}) collective-permute-start(bf16[2,384,128]{2,1,0:T(8,128)(2,1)S(1)} %get-tuple-element.20), channel_id=1, source_target_pairs={{0,1},{1,2},{2,3},{3,0},{4,5},{5,6},{6,7},{7,4},{8,9},{9,10},{10,1... | collective-permute-start | bytes 589832 | tf_op jit(solution)/shard_map/ppermute | solution.py:247
  10.5 0.0 collective-permute-done.h8
  10.5 0.0 collective-permute-done.1.h1
  10.6 0.0 collective-permute-done.2.h9
  10.6 0.7 shard_map.86
  11.2 1.6 %collective-permute-start.3 = (bf16[8,9216]{1,0:T(8,128)(2,1)S(1)}, bf16[8,9216]{1,0:T(8,128)(2,1)S(1)}, u32[]{:S(2)}, u32[]{:S(2)}) collective-permute-start(bf16[8,9216]{1,0:T(8,128)(2,1)S(1)} %get-tuple-element.17), channel_id=1, source_target_pairs={{0,32},{16,48},{32,0},{48,16},{64,96},{80,112},{96,64},{112,80},{1... | collective-permute-start | bytes 442376 | tf_op jit(solution)/shard_map/ppermute | solution.py:237
  12.8 2.7 %collective-permute-start.4 = (bf16[8,9216]{1,0:T(8,128)(2,1)S(1)}, bf16[8,9216]{1,0:T(8,128)(2,1)S(1)}, u32[]{:S(2)}, u32[]{:S(2)}) collective-permute-start(bf16[8,9216]{1,0:T(8,128)(2,1)S(1)} %get-tuple-element.18), channel_id=1, source_target_pairs={{0,64},{16,80},{32,96},{48,112},{64,0},{80,16},{96,32},{112,48},{1... | collective-permute-start | bytes 442376 | tf_op jit(solution)/shard_map/ppermute | solution.py:237
  15.5 0.5 collective-permute-start.5
  16.0 4.5 %collective-permute-start.7 = (bf16[2,384,128]{2,1,0:T(8,128)(2,1)S(1)}, bf16[2,384,128]{2,1,0:T(8,128)(2,1)S(1)}, u32[]{:S(2)}, u32[]{:S(2)}) collective-permute-start(bf16[2,384,128]{2,1,0:T(8,128)(2,1)S(1)} %get-tuple-element.22), channel_id=1, source_target_pairs={{0,2},{1,3},{2,0},{3,1},{4,6},{5,7},{6,4},{7,5},{8,10},{9,11},{10,... | collective-permute-start | bytes 589832 | tf_op jit(solution)/shard_map/ppermute | solution.py:247
  20.5 1.7 %collective-permute-done.6.early.refs_1_ = bf16[2,384,128]{2,1,0:T(8,128)(2,1)S(1)} collective-permute-done((bf16[2,384,128]{2,1,0:T(8,128)(2,1)S(1)}, bf16[2,384,128]{2,1,0:T(8,128)(2,1)S(1)}, u32[]{:S(2)}, u32[]{:S(2)}) %collective-permute-start.6) | collective-permute-done | bytes 196640 | tf_op jit(solution)/shard_map/ppermute | solution.py:247
  22.2 2.4 %collective-permute-start.8 = (bf16[2,384,128]{2,1,0:T(8,128)(2,1)S(1)}, bf16[2,384,128]{2,1,0:T(8,128)(2,1)S(1)}, u32[]{:S(2)}, u32[]{:S(2)}) collective-permute-start(bf16[2,384,128]{2,1,0:T(8,128)(2,1)S(1)} %get-tuple-element.23), channel_id=1, source_target_pairs={{0,3},{1,0},{2,1},{3,2},{4,7},{5,4},{6,5},{7,6},{8,11},{9,8},{10,9... | collective-permute-start | bytes 589832 | tf_op jit(solution)/shard_map/ppermute | solution.py:247
  24.7 2.2 %shard_map.88 = bf16[16,432,128]{2,1,0:T(8,128)(2,1)} custom-call(s32[3]{0:T(128)S(1)} %pad_add_fusion.place, s32[16]{0:T(128)S(1)} %copy-done.6, bf16[128,3072]{1,0:T(8,128)(2,1)S(1)} %bitcast.10, bf16[128,3072]{1,0:T(8,128)(2,1)S(1)} %bitcast.12, bf16[128,3072]{1,0:T(8,128)(2,1)S(1)} %bitcast.14, bf16[8,9216]{1,0:T(8,128)(2,1)S(1)} %get-tuple-element.16.h0, ...), custom_call_target="tpu_custom_call" | custom-call | tf_op jit(solution)/shard_map/pallas_call | solution.py:294
  26.9 9.6 %all-to-all-start = ((bf16[16,432,128]{2,1,0:T(8,128)(2,1)}), bf16[16,432,128]{2,1,0:T(8,128)(2,1)S(1)}, u32[]{:S(2)}, u32[]{:S(2)}) async-start(bf16[16,432,128]{2,1,0:T(8,128)(2,1)} %shard_map.88), calls=%async_computation | async-start | bytes 3538944 | tf_op jit(solution)/shard_map/all_to_all | solution.py:300
  36.5 0.0 copy-start.7
  36.5 0.0 copy-start.8
  36.6 0.6 shard_map.89
  37.2 2.0 %collective-permute-start.9 = (bf16[4,320,128]{2,1,0:T(8,128)(2,1)S(1)}, bf16[4,320,128]{2,1,0:T(8,128)(2,1)S(1)}, u32[]{:S(2)}, u32[]{:S(2)}) collective-permute-start(bf16[4,320,128]{2,1,0:T(8,128)(2,1)S(1)} %get-tuple-element.25), channel_id=1, source_target_pairs={{0,4},{1,5},{2,6},{3,7},{4,8},{5,9},{6,10},{7,11},{8,12},{9,13},{1... | collective-permute-start | bytes 983048 | tf_op jit(solution)/shard_map/ppermute | solution.py:247
  39.2 2.7 %collective-permute-start.10 = (bf16[4,320,128]{2,1,0:T(8,128)(2,1)S(1)}, bf16[4,320,128]{2,1,0:T(8,128)(2,1)S(1)}, u32[]{:S(2)}, u32[]{:S(2)}) collective-permute-start(bf16[4,320,128]{2,1,0:T(8,128)(2,1)S(1)} %get-tuple-element.26), channel_id=1, source_target_pairs={{0,8},{1,9},{2,10},{3,11},{4,12},{5,13},{6,14},{7,15},{8,0},{9,1},... | collective-permute-start | bytes 983048 | tf_op jit(solution)/shard_map/ppermute | solution.py:247
  41.9 1.5 %collective-permute-start.11 = (bf16[4,320,128]{2,1,0:T(8,128)(2,1)S(1)}, bf16[4,320,128]{2,1,0:T(8,128)(2,1)S(1)}, u32[]{:S(2)}, u32[]{:S(2)}) collective-permute-start(bf16[4,320,128]{2,1,0:T(8,128)(2,1)S(1)} %get-tuple-element.27), channel_id=1, source_target_pairs={{0,12},{1,13},{2,14},{3,15},{4,0},{5,1},{6,2},{7,3},{8,4},{9,5},{1... | collective-permute-start | bytes 983048 | tf_op jit(solution)/shard_map/ppermute | solution.py:247
  43.3 17.7 %collective-permute-done.9.p1 = bf16[4,320,128]{2,1,0:T(8,128)(2,1)S(1)} collective-permute-done((bf16[4,320,128]{2,1,0:T(8,128)(2,1)S(1)}, bf16[4,320,128]{2,1,0:T(8,128)(2,1)S(1)}, u32[]{:S(2)}, u32[]{:S(2)}) %collective-permute-start.9) | collective-permute-done | bytes 327712 | tf_op jit(solution)/shard_map/ppermute | solution.py:247
  61.0 8.6 %collective-permute-done.10.p2 = bf16[4,320,128]{2,1,0:T(8,128)(2,1)S(1)} collective-permute-done((bf16[4,320,128]{2,1,0:T(8,128)(2,1)S(1)}, bf16[4,320,128]{2,1,0:T(8,128)(2,1)S(1)}, u32[]{:S(2)}, u32[]{:S(2)}) %collective-permute-start.10) | collective-permute-done | bytes 327712 | tf_op jit(solution)/shard_map/ppermute | solution.py:247
  69.6 10.8 %all-to-all-done.came = bf16[16,432,128]{2,1,0:T(8,128)(2,1)S(1)} async-done(((bf16[16,432,128]{2,1,0:T(8,128)(2,1)}), bf16[16,432,128]{2,1,0:T(8,128)(2,1)S(1)}, u32[]{:S(2)}, u32[]{:S(2)}) %all-to-all-start) | async-done | bytes 1769504 | tf_op jit(solution)/shard_map/all_to_all | solution.py:300
  80.3 11.2 %shard_map.90 = bf16[16,208,128]{2,1,0:T(8,128)(2,1)S(1)} custom-call(s32[3]{0:T(128)S(1)} %pad_add_fusion.place, s32[16]{0:T(128)S(1)} %copy-done.6, s32[16]{0:T(128)S(1)} %copy-done.7, s32[16]{0:T(128)S(1)} %copy-done.8, bf16[16,432,128]{2,1,0:T(8,128)(2,1)S(1)} %all-to-all-done.came, bf16[4,320,128]{2,1,0:T(8,128)(2,1)S(1)} %get-tuple-element.24.p0, ...), custom_call_target="tpu_custom_call" | custom-call | tf_op jit(solution)/shard_map/pallas_call | solution.py:303
  91.6 30.0 %all_to_all.10.returned = bf16[16,208,128]{2,1,0:T(8,128)(2,1)S(1)} all-to-all(bf16[16,208,128]{2,1,0:T(8,128)(2,1)S(1)} %shard_map.90), channel_id=1, replica_groups=mesh['grp'=16,'sp'=16] {'sp'}, dimensions={0} | all-to-all | bytes 1703936 | tf_op jit(solution)/shard_map/all_to_all | solution.py:315
  121.6 1.6 %shard_map.91 = (bf16[128,3072]{1,0:T(8,128)(2,1)}, bf16[8,3072]{1,0:T(8,128)(2,1)}) custom-call(s32[3]{0:T(128)S(1)} %pad_add_fusion.place, s32[16]{0:T(128)S(1)} %copy-done.6, s32[16]{0:T(128)S(1)} %copy-done.7, s32[16]{0:T(128)S(1)} %copy-done.8, bf16[16,208,128]{2,1,0:T(8,128)(2,1)S(1)} %all_to_all.10.returned), custom_call_target="tpu_custom_call" | custom-call | tf_op jit(solution)/shard_map/pallas_call | solution.py:316
  (20 shorter events, 0.0 us)
Async XLA Ops:
  0.6 9.9 %copy-start.6 = (s32[16]{0:T(128)S(1)}, s32[16]{0:T(128)}, u32[]{:S(2)}) copy-start(s32[16]{0:T(128)} %assign.7) | copy-start | bytes 196
  0.6 9.9 %collective-permute-start = (bf16[8,9216]{1,0:T(8,128)(2,1)}, bf16[8,9216]{1,0:T(8,128)(2,1)S(1)}, u32[]{:S(2)}, u32[]{:S(2)}) collective-permute-start(bf16[8,9216]{1,0:T(8,128)(2,1)} %bitcast.15), channel_id=1, source_target_pairs={{0,128},{16,144},{32,160},{48,176},{64,192},{80,208},{96,224},{112... | collective-permute-start | bytes 442376 | tf_op jit(solution)/shard_map/ppermute | solution.py:237
  2.6 8.0 %collective-permute-start.1 = (bf16[8,9216]{1,0:T(8,128)(2,1)}, bf16[8,9216]{1,0:T(8,128)(2,1)S(1)}, u32[]{:S(2)}, u32[]{:S(2)}) collective-permute-start(bf16[8,9216]{1,0:T(8,128)(2,1)} %bitcast.16), channel_id=1, source_target_pairs={{0,16},{16,0},{32,48},{48,32},{64,80},{80,64},{96,112},{112,96},{1... | collective-permute-start | bytes 442376 | tf_op jit(solution)/shard_map/ppermute | solution.py:237
  2.6 8.0 %collective-permute-start.2 = (bf16[8,9216]{1,0:T(8,128)(2,1)}, bf16[8,9216]{1,0:T(8,128)(2,1)S(1)}, u32[]{:S(2)}, u32[]{:S(2)}) collective-permute-start(bf16[8,9216]{1,0:T(8,128)(2,1)} %bitcast.17), channel_id=1, source_target_pairs={{0,144},{16,128},{32,176},{48,160},{64,208},{80,192},{96,240},{112... | collective-permute-start | bytes 442376 | tf_op jit(solution)/shard_map/ppermute | solution.py:237
  2.9 1.1 copy-start
  4.1 1.1 copy-start.2
  5.2 1.1 copy-start.4
  6.3 4.2 %copy-start.5 = (bf16[1,8,9216]{2,1,0:T(8,128)(2,1)S(1)}, bf16[1,8,9216]{2,1,0:T(8,128)(2,1)}, u32[]{:S(2)}) copy-start(bf16[1,8,9216]{2,1,0:T(8,128)(2,1)} %param.10) | copy-start | bytes 442372
  6.3 18.3 %copy-start.1 = (bf16[1,128,3072]{2,1,0:T(8,128)(2,1)S(1)}, bf16[1,128,3072]{2,1,0:T(8,128)(2,1)}, u32[]{:S(2)}) copy-start(bf16[1,128,3072]{2,1,0:T(8,128)(2,1)} %param.7) | copy-start | bytes 2359300
  6.4 18.3 %copy-start.3 = (bf16[1,128,3072]{2,1,0:T(8,128)(2,1)S(1)}, bf16[1,128,3072]{2,1,0:T(8,128)(2,1)}, u32[]{:S(2)}) copy-start(bf16[1,128,3072]{2,1,0:T(8,128)(2,1)} %param.8) | copy-start | bytes 2359300
  7.2 15.0 %collective-permute-start.6 = (bf16[2,384,128]{2,1,0:T(8,128)(2,1)S(1)}, bf16[2,384,128]{2,1,0:T(8,128)(2,1)S(1)}, u32[]{:S(2)}, u32[]{:S(2)}) collective-permute-start(bf16[2,384,128]{2,1,0:T(8,128)(2,1)S(1)} %get-tuple-element.20), channel_id=1, source_target_pairs={{0,1},{1,2},{2,3},{3,0},{4,5},{5,6},{6,7},{7,4},{8,9},{9,10},{10,1... | collective-permute-start | bytes 589832 | tf_op jit(solution)/shard_map/ppermute | solution.py:247
  11.2 13.4 %collective-permute-start.3 = (bf16[8,9216]{1,0:T(8,128)(2,1)S(1)}, bf16[8,9216]{1,0:T(8,128)(2,1)S(1)}, u32[]{:S(2)}, u32[]{:S(2)}) collective-permute-start(bf16[8,9216]{1,0:T(8,128)(2,1)S(1)} %get-tuple-element.17), channel_id=1, source_target_pairs={{0,32},{16,48},{32,0},{48,16},{64,96},{80,112},{96,64},{112,80},{1... | collective-permute-start | bytes 442376 | tf_op jit(solution)/shard_map/ppermute | solution.py:237
  12.8 11.9 %collective-permute-start.4 = (bf16[8,9216]{1,0:T(8,128)(2,1)S(1)}, bf16[8,9216]{1,0:T(8,128)(2,1)S(1)}, u32[]{:S(2)}, u32[]{:S(2)}) collective-permute-start(bf16[8,9216]{1,0:T(8,128)(2,1)S(1)} %get-tuple-element.18), channel_id=1, source_target_pairs={{0,64},{16,80},{32,96},{48,112},{64,0},{80,16},{96,32},{112,48},{1... | collective-permute-start | bytes 442376 | tf_op jit(solution)/shard_map/ppermute | solution.py:237
  15.5 9.1 %collective-permute-start.5 = (bf16[8,9216]{1,0:T(8,128)(2,1)S(1)}, bf16[8,9216]{1,0:T(8,128)(2,1)S(1)}, u32[]{:S(2)}, u32[]{:S(2)}) collective-permute-start(bf16[8,9216]{1,0:T(8,128)(2,1)S(1)} %get-tuple-element.19), channel_id=1, source_target_pairs={{0,96},{16,112},{32,64},{48,80},{64,32},{80,48},{96,0},{112,16},{1... | collective-permute-start | bytes 442376 | tf_op jit(solution)/shard_map/ppermute | solution.py:237
  16.0 20.5 %collective-permute-start.7 = (bf16[2,384,128]{2,1,0:T(8,128)(2,1)S(1)}, bf16[2,384,128]{2,1,0:T(8,128)(2,1)S(1)}, u32[]{:S(2)}, u32[]{:S(2)}) collective-permute-start(bf16[2,384,128]{2,1,0:T(8,128)(2,1)S(1)} %get-tuple-element.22), channel_id=1, source_target_pairs={{0,2},{1,3},{2,0},{3,1},{4,6},{5,7},{6,4},{7,5},{8,10},{9,11},{10,... | collective-permute-start | bytes 589832 | tf_op jit(solution)/shard_map/ppermute | solution.py:247
  22.2 14.3 %collective-permute-start.8 = (bf16[2,384,128]{2,1,0:T(8,128)(2,1)S(1)}, bf16[2,384,128]{2,1,0:T(8,128)(2,1)S(1)}, u32[]{:S(2)}, u32[]{:S(2)}) collective-permute-start(bf16[2,384,128]{2,1,0:T(8,128)(2,1)S(1)} %get-tuple-element.23), channel_id=1, source_target_pairs={{0,3},{1,0},{2,1},{3,2},{4,7},{5,4},{6,5},{7,6},{8,11},{9,8},{10,9... | collective-permute-start | bytes 589832 | tf_op jit(solution)/shard_map/ppermute | solution.py:247
  26.9 53.5 %all-to-all-start = ((bf16[16,432,128]{2,1,0:T(8,128)(2,1)}), bf16[16,432,128]{2,1,0:T(8,128)(2,1)S(1)}, u32[]{:S(2)}, u32[]{:S(2)}) async-start(bf16[16,432,128]{2,1,0:T(8,128)(2,1)} %shard_map.88), calls=%async_computation | async-start | bytes 3538944 | tf_op jit(solution)/shard_map/all_to_all | solution.py:300
  36.5 43.8 %copy-start.7 = (s32[16]{0:T(128)S(1)}, s32[16]{0:T(128)}, u32[]{:S(2)}) copy-start(s32[16]{0:T(128)} %prompt_len.3) | copy-start | bytes 196
  36.5 43.8 %copy-start.8 = (s32[16]{0:T(128)S(1)}, s32[16]{0:T(128)}, u32[]{:S(2)}) copy-start(s32[16]{0:T(128)} %ref_count.3) | copy-start | bytes 196
  37.2 23.8 %collective-permute-start.9 = (bf16[4,320,128]{2,1,0:T(8,128)(2,1)S(1)}, bf16[4,320,128]{2,1,0:T(8,128)(2,1)S(1)}, u32[]{:S(2)}, u32[]{:S(2)}) collective-permute-start(bf16[4,320,128]{2,1,0:T(8,128)(2,1)S(1)} %get-tuple-element.25), channel_id=1, source_target_pairs={{0,4},{1,5},{2,6},{3,7},{4,8},{5,9},{6,10},{7,11},{8,12},{9,13},{1... | collective-permute-start | bytes 983048 | tf_op jit(solution)/shard_map/ppermute | solution.py:247
  39.2 30.4 %collective-permute-start.10 = (bf16[4,320,128]{2,1,0:T(8,128)(2,1)S(1)}, bf16[4,320,128]{2,1,0:T(8,128)(2,1)S(1)}, u32[]{:S(2)}, u32[]{:S(2)}) collective-permute-start(bf16[4,320,128]{2,1,0:T(8,128)(2,1)S(1)} %get-tuple-element.26), channel_id=1, source_target_pairs={{0,8},{1,9},{2,10},{3,11},{4,12},{5,13},{6,14},{7,15},{8,0},{9,1},... | collective-permute-start | bytes 983048 | tf_op jit(solution)/shard_map/ppermute | solution.py:247
  41.9 27.7 %collective-permute-start.11 = (bf16[4,320,128]{2,1,0:T(8,128)(2,1)S(1)}, bf16[4,320,128]{2,1,0:T(8,128)(2,1)S(1)}, u32[]{:S(2)}, u32[]{:S(2)}) collective-permute-start(bf16[4,320,128]{2,1,0:T(8,128)(2,1)S(1)} %get-tuple-element.27), channel_id=1, source_target_pairs={{0,12},{1,13},{2,14},{3,15},{4,0},{5,1},{6,2},{7,3},{8,4},{9,5},{1... | collective-permute-start | bytes 983048 | tf_op jit(solution)/shard_map/ppermute | solution.py:247

commit v3 on v2

--- a/solution.py
+++ b/solution.py
@@ -10,21 +10,21 @@
 
 HD = 128
 SIDE = 4
+EARLY = 3
 NEG_FILL = -1e30
 FLOPS_S = 30000000000
-KEY_SPAN = 512
 FACTOR = math.log2(math.e) / math.sqrt(HD)
 VMEM_LIMIT = 48 * 1024 * 1024
 VMEM = pl.BlockSpec(memory_space=pltpu.VMEM)
 SMEM = pl.BlockSpec(memory_space=pltpu.SMEM)
-HBM = pl.BlockSpec(memory_space=pltpu.HBM)
-
-
-def call(body, out_shape, in_specs, out_specs, scratch_shapes=(), grid=(), cost=None):
+
+
+def call(body, out_shape, in_specs, out_specs, scratch_shapes=(), grid=(), cost=None, aliases={}):
     return pl.pallas_call(
         body,
         grid=grid,
         cost_estimate=cost,
+        input_output_aliases=aliases,
         out_shape=out_shape,
         in_specs=in_specs,
         out_specs=out_specs,
@@ -68,42 +68,35 @@
     return y * SIDE + z
 
 
-def fetch(refs, columns, held, sems):
-    copies = [pltpu.make_async_copy(ref.at[:, columns], held.at[part], sems.at[part]) for part, ref in enumerate(refs)]
-    for copy in copies:
-        copy.start()
-    for copy in copies:
-        copy.wait()
-
-
-def pack_shared(plan, place, q, k, v, *rest):
-    rows, first = plan.rows, plan.shards * HD
-    outs, (held, sems) = rest[:SIDE], rest[SIDE:]
-    fetch((q, k, v), slice(first, plan.heads * HD), held, sems)
+def pack_shared(plan, place, q, k, v, *outs):
+    rows = plan.rows
     for dz in range(SIDE):
         z = lax.rem(place[2] + dz, SIDE)
         for pair in range(2):
-            for part in range(3):
-                outs[dz][pair, part * rows : (part + 1) * rows, :] = held[part, :, head_at(pair * SIDE + z)]
-
-
-def pack_whole(plan, place, assign, q, k, v, h0, h2, h4, h6, early, out):
+            for part, ref in enumerate((q, k, v)):
+                outs[dz][pair, part * rows : (part + 1) * rows, :] = ref[:, head_at(plan.shards + pair * SIDE + z)]
+
+
+def pack_whole(plan, q, k, v, out):
     rows = plan.rows
+    for device in range(plan.shards):
+        for part, ref in enumerate((q, k, v)):
+            out[device, part * rows : (part + 1) * rows, :] = ref[:, head(device)]
+
+
+def pack_text(plan, place, assign, h0, h2, h4, h6, early, also, whole, out):
     owner = jnp.int32(0)
     for request in range(1, plan.groups):
         owner = jnp.where(assign[request] == place[0], request, owner)
     came = lax.rem(lax.div(lax.bitwise_xor(owner, place[0]), 2), 4)
-    for device in range(plan.shards):
-        for part, ref in enumerate((q, k, v)):
-            out[device, part * rows : (part + 1) * rows, :] = ref[:, head(device)]
-        pieces = []
-        for own in (device, plan.shared(device)):
-            for part in range(3):
-                at = head(part * plan.heads + own)
-                low = jnp.where(came == 0, h0[:, at].astype(jnp.float32), h2[:, at].astype(jnp.float32))
-                high = jnp.where(came == 2, h4[:, at].astype(jnp.float32), h6[:, at].astype(jnp.float32))
-                pieces.append(jnp.where(came < 2, low, high))
-        out[device, 3 * rows :, :] = jnp.concatenate(pieces, axis=0).astype(jnp.bfloat16)
+    for turn, ref in enumerate((h0, h2, h4, h6)):
+
+        @pl.when(came == turn)
+        def _(ref=ref):
+            for device in range(plan.shards):
+                both = (device, plan.shared(device))
+                pieces = [ref[:, head(part * plan.heads + own)].astype(jnp.float32) for own in both for part in range(3)]
+                out[device, :, :] = jnp.concatenate(pieces, axis=0).astype(jnp.bfloat16)
 
 
 def choose(place, assign, h0, h8, h1, h9, *outs):
@@ -162,22 +155,15 @@
 
 
 def attend(queries, pieces):
-    mixed = top = None
-    for keys, values, alive in pieces:
-        score = scores(queries, keys)
-        if alive is not None:
-            score = jnp.where(alive, score, NEG_FILL)
-        higher = largest(score)
-        if top is not None:
-            higher = jnp.maximum(top, higher)
-        part = total(weights(score, higher), values)
-        mixed = part if top is None else mixed * jnp.exp2((top - higher) * FACTOR) + part
-        top = higher
+    parts = [scores(queries, keys) for keys, _, _ in pieces]
+    parts = [part if alive is None else jnp.where(alive, part, NEG_FILL) for part, (_, _, alive) in zip(parts, pieces)]
+    top = functools.reduce(jnp.maximum, [largest(part) for part in parts])
+    mixed = sum(total(weights(part, top), values) for part, (_, values, _) in zip(parts, pieces))
     return (mixed[:, :HD] / mixed[:, HD:]).astype(jnp.bfloat16)
 
 
-def attention(plan, place, assign, prompt_len, ref_count, came, p0, p1, p2, p3, out, keys, values, texts, text_values):
-    rows, half, images, text_rows, slots = plan.rows, plan.half, plan.images, plan.text_rows, plan.slots
+def attention(plan, place, assign, prompt_len, ref_count, came, p0, p1, p2, p3, out, texts):
+    rows, half, text_rows, slots = plan.rows, plan.half, plan.text_rows, plan.slots
     alive = is_alive(plan, lax.broadcasted_iota(jnp.int32, (1, slots), 1), owner_counts(plan, place, assign, prompt_len, ref_count))
     parts = (p0, p1, p2, p3)
     for source in range(0, plan.shards, 2):
@@ -185,25 +171,24 @@
         at = source * text_rows
         for kind in range(6):
             cut = slice(kind * text_rows, (kind + 1) * text_rows)
-            both = jnp.concatenate([one[cut] for one in pair], axis=0).astype(jnp.bfloat16)
-            if kind in (2, 5):
-                text_values[kind // 3, at : at + 2 * text_rows, :HD] = both
+            texts[kind, at : at + 2 * text_rows, :] = jnp.concatenate([one[cut] for one in pair], axis=0).astype(jnp.bfloat16)
+
+    def with_ones(values):
+        return jnp.concatenate([values, jnp.ones_like(values)], axis=1)
+
+    def pieces(which):
+        for block in range(SIDE):
+            if which == 0:
+                mine, at = came.at[block * SIDE : (block + 1) * SIDE], rows
             else:
-                texts[kind, at : at + 2 * text_rows, :] = both
-    text_values[:, :, HD:] = jnp.ones((2, slots, HD), jnp.bfloat16)
-    for source in range(plan.shards):
-        at = slice(source * rows, (source + 1) * rows)
-        keys[0, at, :] = came[source, rows : 2 * rows, :]
-        values[0, at, :HD] = came[source, 2 * rows : 3 * rows, :]
-        part, dz = parts[source // SIDE], source % SIDE
-        keys[1, at, :] = part[dz, half : half + rows, :]
-        values[1, at, :HD] = part[dz, half + rows :, :]
-    values[:, :, HD:] = jnp.ones((2, images, HD), jnp.bfloat16)
+                mine, at = parts[block], half
+            keys = mine[:, at : at + rows, :].reshape(SIDE * rows, HD)
+            values = mine[:, at + rows : at + 2 * rows, :].reshape(SIDE * rows, HD)
+            yield keys, with_ones(values), None
+        yield texts[3 * which + 1], with_ones(texts[3 * which + 2]), alive
 
     def mix(which, queries):
-        cuts = [slice(at, at + KEY_SPAN) for at in range(0, images, KEY_SPAN)]
-        pieces = [(keys[which, cut, :], values[which, cut, :], None) for cut in cuts]
-        return attend(queries, pieces + [(texts[3 * which + 1], text_values[which], alive)])
+        return attend(queries, list(pieces(which)))
 
     for source in range(0, plan.shards, 2):
         mixed = mix(0, came[source : source + 2, 0:rows, :].reshape(2 * rows, HD))
@@ -271,16 +256,14 @@
         return jax.ShapeDtypeStruct(shape, dtype)
 
     images = (img_q[0], img_k[0], img_v[0])
-    shared = width - shards * HD
     parts = call(
         functools.partial(pack_shared, plan),
         (like(2, 3 * rows, HD),) * SIDE,
-        [SMEM] + [HBM] * 3,
+        [SMEM] + [VMEM] * 3,
         (VMEM,) * SIDE,
-        [pltpu.VMEM((3, rows, shared), dtype), pltpu.SemaphoreType.DMA((3,))],
     )(place, *images)
     parts = along_z(parts, shards)
-    early = parts[1]
+    early = (parts[1], parts[EARLY])
     parts = call(
         functools.partial(regroup_shared, plan),
         (like(SIDE, half + 2 * rows, HD),) * SIDE,
@@ -291,12 +274,25 @@
     parts = along_y(parts, shards)
 
     texts = route(plan, place, assign, cond_rows[0])
+    block = (shards, 3 * rows, HD)
+    shape = like(shards, 3 * rows + 6 * text_rows, HD)
     whole = call(
         functools.partial(pack_whole, plan),
-        like(shards, 3 * rows + 6 * text_rows, HD),
-        [SMEM] * 2 + [VMEM] * 7 + [pl.BlockSpec(memory_space=pl.ANY)],
-        VMEM,
-    )(place, assign, *images, *texts, early)
+        shape,
+        [pl.BlockSpec((rows, width), lambda i: (0, 0))] * 3,
+        pl.BlockSpec(block, lambda i: (0, 0, 0)),
+        grid=(1,),
+    )(*images)
+    anywhere = pl.BlockSpec(memory_space=pl.ANY)
+    packet = pl.BlockSpec((text_rows, 3 * width), lambda i: (0, 0))
+    whole = call(
+        functools.partial(pack_text, plan),
+        shape,
+        [SMEM] * 2 + [packet] * SIDE + [anywhere] * 3,
+        pl.BlockSpec((shards, 6 * text_rows, HD), lambda i: (0, 3 * rows // (6 * text_rows), 0)),
+        grid=(1,),
+        aliases={8: 0},
+    )(place, assign, *texts, *early, whole)
     whole = lax.all_to_all(whole, "sp", split_axis=0, concat_axis=0, tiled=True)
 
     lengths = (assign, prompt_len, ref_count)
@@ -306,10 +302,7 @@
         [SMEM] * 4 + [VMEM] * 5,
         VMEM,
         [
-            pltpu.VMEM((2, plan.images, HD), dtype),
-            pltpu.VMEM((2, plan.images, 2 * HD), dtype),
             pltpu.VMEM((6, plan.slots, HD), dtype),
-            pltpu.VMEM((2, plan.slots, 2 * HD), dtype),
         ],
     )(place, *lengths, whole, *parts)
     returned = lax.all_to_all(mixed, "sp", split_axis=0, concat_axis=0, tiled=True)

time: 124 us -> 123 us (level)
  starting transfers between devices: 33.1 us -> 29.7 us
  waiting for transfers between devices: 38.7 us -> 41.6 us
    ppermute x6, starting transfers between devices: 16.4 us -> 14.2 us  [shift(): return lax.ppermute(data, 'sp', pairs)]
    ppermute x6, waiting for transfers between devices: 28 us -> 29.8 us  [shift(): return lax.ppermute(data, 'sp', pairs)]
    unnamed x18 -> x20, local copies, waits for them, and re-layouts: 3.43 us -> 4.33 us
    pallas_call x1 -> x2, Pallas kernels: 2.16 us -> 2.75 us  [the longest x1 1.46 us: on_device(): call(functools.partial(pack_whole, plan), shape, [pl.BlockSpec((rows, wid...]
  transfers between devices with their start and end apart: 13 -> 13, of which waited for: 4 -> 6; matrix products, arithmetic and copies ran while one was open for 0% -> 0% of each run, Pallas kernels for 3% -> 4%
where the time goes in v3:
time: 123 us; the launch traced here: 122 us
  waiting for transfers between devices  41.6 us (34%)
  starting transfers between devices  29.7 us (24%)
  blocking collectives  29.1 us (24%)
  Pallas kernels  16.8 us (14%)
  local copies, waits for them, and re-layouts  4.33 us (4%)
    ppermute x6, waiting for transfers between devices, shift(): return lax.ppermute(data, 'sp', pairs)  29.8 us
    all_to_all x1, blocking collectives, on_device(): lax.all_to_all(mixed, 'sp', split_axis=0, concat_axis=0, tiled=True)  29.1 us
    ppermute x6, starting transfers between devices, shift(): return lax.ppermute(data, 'sp', pairs)  14.2 us
    all_to_all x1, waiting for transfers between devices, on_device(): whole = lax.all_to_all(whole, 'sp', split_axis=0, concat_axis=0, tiled=True)  10.7 us
    pallas_call x1, Pallas kernels, on_device(): call(functools.partial(attention, plan), like(shards, rows + half + 2 * t...  10.4 us
    all_to_all x1, starting transfers between devices, on_device(): whole = lax.all_to_all(whole, 'sp', split_axis=0, concat_axis=0, tiled=True)  8.51 us
    ppermute x6, starting transfers between devices, exchange(): lax.ppermute(data, 'grp', [(i, i ^ bits) for i in range(plan.groups)])  7.01 us
    unnamed x20, local copies, waits for them, and re-layouts  4.33 us
  transfers between devices with their start and end apart: 13, of which 6 were waited for; matrix products, arithmetic and copies ran while one was open for 0% of the time, Pallas kernels for 4%

profile of v3, /device:TPU:32, one launch (start us, length us, event | category | flops | bytes accessed | tf_op | source)
XLA Modules:
  0.0 122.4 jit_solution(10944432869321087343)
XLA Ops:
  0.6 1.9 %collective-permute-start = (bf16[8,9216]{1,0:T(8,128)(2,1)}, bf16[8,9216]{1,0:T(8,128)(2,1)S(1)}, u32[]{:S(2)}, u32[]{:S(2)}) collective-permute-start(bf16[8,9216]{1,0:T(8,128)(2,1)} %bitcast.15), channel_id=1, source_target_pairs={{0,128},{16,144},{32,160},{48,176},{64,192},{80,208},{96,224},{112... | collective-permute-start | bytes 442376 | tf_op jit(solution)/shard_map/ppermute | solution.py:222
  2.6 0.3 collective-permute-start.2
  2.9 0.1 pad_add_fusion.place
  2.9 1.1 copy-done
  4.1 1.1 copy-done.2
  5.2 1.1 copy-done.4
  6.4 0.8 shard_map.87
  7.1 3.3 %collective-permute-start.6 = (bf16[2,384,128]{2,1,0:T(8,128)(2,1)S(1)}, bf16[2,384,128]{2,1,0:T(8,128)(2,1)S(1)}, u32[]{:S(2)}, u32[]{:S(2)}) collective-permute-start(bf16[2,384,128]{2,1,0:T(8,128)(2,1)S(1)} %get-tuple-element.20), channel_id=1, source_target_pairs={{0,1},{1,2},{2,3},{3,0},{4,5},{5,6},{6,7},{7,4},{8,9},{9,10},{10,1... | collective-permute-start | bytes 589832 | tf_op jit(solution)/shard_map/ppermute | solution.py:232
  10.5 2.2 %collective-permute-start.7 = (bf16[2,384,128]{2,1,0:T(8,128)(2,1)S(1)}, bf16[2,384,128]{2,1,0:T(8,128)(2,1)S(1)}, u32[]{:S(2)}, u32[]{:S(2)}) collective-permute-start(bf16[2,384,128]{2,1,0:T(8,128)(2,1)S(1)} %get-tuple-element.21), channel_id=1, source_target_pairs={{0,3},{1,0},{2,1},{3,2},{4,7},{5,4},{6,5},{7,6},{8,11},{9,8},{10,9... | collective-permute-start | bytes 589832 | tf_op jit(solution)/shard_map/ppermute | solution.py:232
  12.7 0.9 copy-done.6
  13.6 0.7 shard_map.86
  14.3 1.6 %collective-permute-start.3 = (bf16[8,9216]{1,0:T(8,128)(2,1)S(1)}, bf16[8,9216]{1,0:T(8,128)(2,1)S(1)}, u32[]{:S(2)}, u32[]{:S(2)}) collective-permute-start(bf16[8,9216]{1,0:T(8,128)(2,1)S(1)} %get-tuple-element.17), channel_id=1, source_target_pairs={{0,32},{16,48},{32,0},{48,16},{64,96},{80,112},{96,64},{112,80},{1... | collective-permute-start | bytes 442376 | tf_op jit(solution)/shard_map/ppermute | solution.py:222
  15.9 2.7 %collective-permute-start.4 = (bf16[8,9216]{1,0:T(8,128)(2,1)S(1)}, bf16[8,9216]{1,0:T(8,128)(2,1)S(1)}, u32[]{:S(2)}, u32[]{:S(2)}) collective-permute-start(bf16[8,9216]{1,0:T(8,128)(2,1)S(1)} %get-tuple-element.18), channel_id=1, source_target_pairs={{0,64},{16,80},{32,96},{48,112},{64,0},{80,16},{96,32},{112,48},{1... | collective-permute-start | bytes 442376 | tf_op jit(solution)/shard_map/ppermute | solution.py:222
  18.6 0.5 collective-permute-start.5
  19.1 2.8 %collective-permute-done.6.early.refs_1_ = bf16[2,384,128]{2,1,0:T(8,128)(2,1)S(1)} collective-permute-done((bf16[2,384,128]{2,1,0:T(8,128)(2,1)S(1)}, bf16[2,384,128]{2,1,0:T(8,128)(2,1)S(1)}, u32[]{:S(2)}, u32[]{:S(2)}) %collective-permute-start.6) | collective-permute-done | bytes 196640 | tf_op jit(solution)/shard_map/ppermute | solution.py:232
  21.9 3.1 %collective-permute-start.8 = (bf16[2,384,128]{2,1,0:T(8,128)(2,1)S(1)}, bf16[2,384,128]{2,1,0:T(8,128)(2,1)S(1)}, u32[]{:S(2)}, u32[]{:S(2)}) collective-permute-start(bf16[2,384,128]{2,1,0:T(8,128)(2,1)S(1)} %get-tuple-element.23), channel_id=1, source_target_pairs={{0,2},{1,3},{2,0},{3,1},{4,6},{5,7},{6,4},{7,5},{8,10},{9,11},{10,... | collective-permute-start | bytes 589832 | tf_op jit(solution)/shard_map/ppermute | solution.py:232
  25.0 1.5 %shard_map.88.whole = bf16[16,432,128]{2,1,0:T(8,128)(2,1)} custom-call(bf16[128,3072]{1,0:T(8,128)(2,1)S(1)} %bitcast.10, bf16[128,3072]{1,0:T(8,128)(2,1)S(1)} %bitcast.12, bf16[128,3072]{1,0:T(8,128)(2,1)S(1)} %bitcast.14), custom_call_target="tpu_custom_call" | custom-call | tf_op jit(solution)/shard_map/pallas_call | solution.py:279
  26.5 1.0 collective-permute-done.5.h6
  27.5 1.3 %shard_map.89 = bf16[16,432,128]{2,1,0:T(8,128)(2,1)} custom-call(s32[3]{0:T(128)S(1)} %pad_add_fusion.place, s32[16]{0:T(128)S(1)} %copy-done.7, bf16[8,9216]{1,0:T(8,128)(2,1)S(1)} %get-tuple-element.16.h0, bf16[8,9216]{1,0:T(8,128)(2,1)S(1)} %collective-permute-done.3.h2, ...), custom_call_target="tpu_custom_call", output_to_operand_aliasing={{}: (8, {})} | custom-call | tf_op jit(solution)/shard_map/pallas_call | solution.py:288
  28.8 8.5 %all-to-all-start = ((bf16[16,432,128]{2,1,0:T(8,128)(2,1)}), bf16[16,432,128]{2,1,0:T(8,128)(2,1)S(1)}, u32[]{:S(2)}, u32[]{:S(2)}) async-start(bf16[16,432,128]{2,1,0:T(8,128)(2,1)} %shard_map.89), calls=%async_computation | async-start | bytes 3538944 | tf_op jit(solution)/shard_map/all_to_all | solution.py:296
  37.3 0.0 copy-start.9
  37.3 0.6 shard_map.90
  38.0 3.5 %collective-permute-start.10 = (bf16[4,320,128]{2,1,0:T(8,128)(2,1)S(1)}, bf16[4,320,128]{2,1,0:T(8,128)(2,1)S(1)}, u32[]{:S(2)}, u32[]{:S(2)}) collective-permute-start(bf16[4,320,128]{2,1,0:T(8,128)(2,1)S(1)} %get-tuple-element.26), channel_id=1, source_target_pairs={{0,8},{1,9},{2,10},{3,11},{4,12},{5,13},{6,14},{7,15},{8,0},{9,1},... | collective-permute-start | bytes 983048 | tf_op jit(solution)/shard_map/ppermute | solution.py:232
  41.5 1.2 collective-permute-start.11
  42.7 0.9 collective-permute-start.9
  43.5 18.8 %collective-permute-done.10.p2 = bf16[4,320,128]{2,1,0:T(8,128)(2,1)S(1)} collective-permute-done((bf16[4,320,128]{2,1,0:T(8,128)(2,1)S(1)}, bf16[4,320,128]{2,1,0:T(8,128)(2,1)S(1)}, u32[]{:S(2)}, u32[]{:S(2)}) %collective-permute-start.10) | collective-permute-done | bytes 327712 | tf_op jit(solution)/shard_map/ppermute | solution.py:232
  62.3 5.0 %collective-permute-done.11.p3 = bf16[4,320,128]{2,1,0:T(8,128)(2,1)S(1)} collective-permute-done((bf16[4,320,128]{2,1,0:T(8,128)(2,1)S(1)}, bf16[4,320,128]{2,1,0:T(8,128)(2,1)S(1)}, u32[]{:S(2)}, u32[]{:S(2)}) %collective-permute-start.11) | collective-permute-done | bytes 327712 | tf_op jit(solution)/shard_map/ppermute | solution.py:232
  67.3 3.3 %collective-permute-done.9.p1 = bf16[4,320,128]{2,1,0:T(8,128)(2,1)S(1)} collective-permute-done((bf16[4,320,128]{2,1,0:T(8,128)(2,1)S(1)}, bf16[4,320,128]{2,1,0:T(8,128)(2,1)S(1)}, u32[]{:S(2)}, u32[]{:S(2)}) %collective-permute-start.9) | collective-permute-done | bytes 327712 | tf_op jit(solution)/shard_map/ppermute | solution.py:232
  70.6 10.7 %all-to-all-done.came = bf16[16,432,128]{2,1,0:T(8,128)(2,1)S(1)} async-done(((bf16[16,432,128]{2,1,0:T(8,128)(2,1)}), bf16[16,432,128]{2,1,0:T(8,128)(2,1)S(1)}, u32[]{:S(2)}, u32[]{:S(2)}) %all-to-all-start) | async-done | bytes 1769504 | tf_op jit(solution)/shard_map/all_to_all | solution.py:296
  81.3 10.4 %shard_map.91 = bf16[16,208,128]{2,1,0:T(8,128)(2,1)S(1)} custom-call(s32[3]{0:T(128)S(1)} %pad_add_fusion.place, s32[16]{0:T(128)S(1)} %copy-done.7, s32[16]{0:T(128)S(1)} %copy-done.8, s32[16]{0:T(128)S(1)} %copy-done.9, bf16[16,432,128]{2,1,0:T(8,128)(2,1)S(1)} %all-to-all-done.came, bf16[4,320,128]{2,1,0:T(8,128)(2,1)S(1)} %get-tuple-element.24.p0, ...), custom_call_target="tpu_custom_call" | custom-call | tf_op jit(solution)/shard_map/pallas_call | solution.py:299
  91.6 29.1 %all_to_all.10.returned = bf16[16,208,128]{2,1,0:T(8,128)(2,1)S(1)} all-to-all(bf16[16,208,128]{2,1,0:T(8,128)(2,1)S(1)} %shard_map.91), channel_id=1, replica_groups=mesh['grp'=16,'sp'=16] {'sp'}, dimensions={0} | all-to-all | bytes 1703936 | tf_op jit(solution)/shard_map/all_to_all | solution.py:308
  120.7 1.6 %shard_map.92 = (bf16[128,3072]{1,0:T(8,128)(2,1)}, bf16[8,3072]{1,0:T(8,128)(2,1)}) custom-call(s32[3]{0:T(128)S(1)} %pad_add_fusion.place, s32[16]{0:T(128)S(1)} %copy-done.7, s32[16]{0:T(128)S(1)} %copy-done.8, s32[16]{0:T(128)S(1)} %copy-done.9, bf16[16,208,128]{2,1,0:T(8,128)(2,1)S(1)} %all_to_all.10.returned), custom_call_target="tpu_custom_call" | custom-call | tf_op jit(solution)/shard_map/pallas_call | solution.py:309
  (23 shorter events, 0.1 us)
Async XLA Ops:
  0.6 12.1 %copy-start.7 = (s32[16]{0:T(128)S(1)}, s32[16]{0:T(128)}, u32[]{:S(2)}) copy-start(s32[16]{0:T(128)} %assign.7) | copy-start | bytes 196
  0.6 12.0 %collective-permute-start = (bf16[8,9216]{1,0:T(8,128)(2,1)}, bf16[8,9216]{1,0:T(8,128)(2,1)S(1)}, u32[]{:S(2)}, u32[]{:S(2)}) collective-permute-start(bf16[8,9216]{1,0:T(8,128)(2,1)} %bitcast.15), channel_id=1, source_target_pairs={{0,128},{16,144},{32,160},{48,176},{64,192},{80,208},{96,224},{112... | collective-permute-start | bytes 442376 | tf_op jit(solution)/shard_map/ppermute | solution.py:222
  2.6 10.1 %collective-permute-start.1 = (bf16[8,9216]{1,0:T(8,128)(2,1)}, bf16[8,9216]{1,0:T(8,128)(2,1)S(1)}, u32[]{:S(2)}, u32[]{:S(2)}) collective-permute-start(bf16[8,9216]{1,0:T(8,128)(2,1)} %bitcast.16), channel_id=1, source_target_pairs={{0,16},{16,0},{32,48},{48,32},{64,80},{80,64},{96,112},{112,96},{1... | collective-permute-start | bytes 442376 | tf_op jit(solution)/shard_map/ppermute | solution.py:222
  2.6 10.1 %collective-permute-start.2 = (bf16[8,9216]{1,0:T(8,128)(2,1)}, bf16[8,9216]{1,0:T(8,128)(2,1)S(1)}, u32[]{:S(2)}, u32[]{:S(2)}) collective-permute-start(bf16[8,9216]{1,0:T(8,128)(2,1)} %bitcast.17), channel_id=1, source_target_pairs={{0,144},{16,128},{32,176},{48,160},{64,208},{80,192},{96,240},{112... | collective-permute-start | bytes 442376 | tf_op jit(solution)/shard_map/ppermute | solution.py:222
  2.9 1.1 copy-start
  4.1 1.1 copy-start.2
  5.2 1.1 copy-start.4
  6.3 18.6 %copy-start.1 = (bf16[1,128,3072]{2,1,0:T(8,128)(2,1)S(1)}, bf16[1,128,3072]{2,1,0:T(8,128)(2,1)}, u32[]{:S(2)}) copy-start(bf16[1,128,3072]{2,1,0:T(8,128)(2,1)} %param.7) | copy-start | bytes 2359300
  6.3 18.6 %copy-start.3 = (bf16[1,128,3072]{2,1,0:T(8,128)(2,1)S(1)}, bf16[1,128,3072]{2,1,0:T(8,128)(2,1)}, u32[]{:S(2)}) copy-start(bf16[1,128,3072]{2,1,0:T(8,128)(2,1)} %param.8) | copy-start | bytes 2359300
  6.4 18.6 %copy-start.5 = (bf16[1,128,3072]{2,1,0:T(8,128)(2,1)S(1)}, bf16[1,128,3072]{2,1,0:T(8,128)(2,1)}, u32[]{:S(2)}) copy-start(bf16[1,128,3072]{2,1,0:T(8,128)(2,1)} %param.9) | copy-start | bytes 2359300
  7.1 14.8 %collective-permute-start.6 = (bf16[2,384,128]{2,1,0:T(8,128)(2,1)S(1)}, bf16[2,384,128]{2,1,0:T(8,128)(2,1)S(1)}, u32[]{:S(2)}, u32[]{:S(2)}) collective-permute-start(bf16[2,384,128]{2,1,0:T(8,128)(2,1)S(1)} %get-tuple-element.20), channel_id=1, source_target_pairs={{0,1},{1,2},{2,3},{3,0},{4,5},{5,6},{6,7},{7,4},{8,9},{9,10},{10,1... | collective-permute-start | bytes 589832 | tf_op jit(solution)/shard_map/ppermute | solution.py:232
  10.5 16.0 %collective-permute-start.7 = (bf16[2,384,128]{2,1,0:T(8,128)(2,1)S(1)}, bf16[2,384,128]{2,1,0:T(8,128)(2,1)S(1)}, u32[]{:S(2)}, u32[]{:S(2)}) collective-permute-start(bf16[2,384,128]{2,1,0:T(8,128)(2,1)S(1)} %get-tuple-element.21), channel_id=1, source_target_pairs={{0,3},{1,0},{2,1},{3,2},{4,7},{5,4},{6,5},{7,6},{8,11},{9,8},{10,9... | collective-permute-start | bytes 589832 | tf_op jit(solution)/shard_map/ppermute | solution.py:232
  12.7 0.9 copy-start.6
  14.3 12.2 %collective-permute-start.3 = (bf16[8,9216]{1,0:T(8,128)(2,1)S(1)}, bf16[8,9216]{1,0:T(8,128)(2,1)S(1)}, u32[]{:S(2)}, u32[]{:S(2)}) collective-permute-start(bf16[8,9216]{1,0:T(8,128)(2,1)S(1)} %get-tuple-element.17), channel_id=1, source_target_pairs={{0,32},{16,48},{32,0},{48,16},{64,96},{80,112},{96,64},{112,80},{1... | collective-permute-start | bytes 442376 | tf_op jit(solution)/shard_map/ppermute | solution.py:222
  15.9 10.6 %collective-permute-start.4 = (bf16[8,9216]{1,0:T(8,128)(2,1)S(1)}, bf16[8,9216]{1,0:T(8,128)(2,1)S(1)}, u32[]{:S(2)}, u32[]{:S(2)}) collective-permute-start(bf16[8,9216]{1,0:T(8,128)(2,1)S(1)} %get-tuple-element.18), channel_id=1, source_target_pairs={{0,64},{16,80},{32,96},{48,112},{64,0},{80,16},{96,32},{112,48},{1... | collective-permute-start | bytes 442376 | tf_op jit(solution)/shard_map/ppermute | solution.py:222
  18.6 8.9 %collective-permute-start.5 = (bf16[8,9216]{1,0:T(8,128)(2,1)S(1)}, bf16[8,9216]{1,0:T(8,128)(2,1)S(1)}, u32[]{:S(2)}, u32[]{:S(2)}) collective-permute-start(bf16[8,9216]{1,0:T(8,128)(2,1)S(1)} %get-tuple-element.19), channel_id=1, source_target_pairs={{0,96},{16,112},{32,64},{48,80},{64,32},{80,48},{96,0},{112,16},{1... | collective-permute-start | bytes 442376 | tf_op jit(solution)/shard_map/ppermute | solution.py:222
  21.9 15.4 %collective-permute-start.8 = (bf16[2,384,128]{2,1,0:T(8,128)(2,1)S(1)}, bf16[2,384,128]{2,1,0:T(8,128)(2,1)S(1)}, u32[]{:S(2)}, u32[]{:S(2)}) collective-permute-start(bf16[2,384,128]{2,1,0:T(8,128)(2,1)S(1)} %get-tuple-element.23), channel_id=1, source_target_pairs={{0,2},{1,3},{2,0},{3,1},{4,6},{5,7},{6,4},{7,5},{8,10},{9,11},{10,... | collective-permute-start | bytes 589832 | tf_op jit(solution)/shard_map/ppermute | solution.py:232
  28.8 52.5 %all-to-all-start = ((bf16[16,432,128]{2,1,0:T(8,128)(2,1)}), bf16[16,432,128]{2,1,0:T(8,128)(2,1)S(1)}, u32[]{:S(2)}, u32[]{:S(2)}) async-start(bf16[16,432,128]{2,1,0:T(8,128)(2,1)} %shard_map.89), calls=%async_computation | async-start | bytes 3538944 | tf_op jit(solution)/shard_map/all_to_all | solution.py:296
  37.3 44.0 %copy-start.8 = (s32[16]{0:T(128)S(1)}, s32[16]{0:T(128)}, u32[]{:S(2)}) copy-start(s32[16]{0:T(128)} %prompt_len.3) | copy-start | bytes 196
  37.3 43.9 %copy-start.9 = (s32[16]{0:T(128)S(1)}, s32[16]{0:T(128)}, u32[]{:S(2)}) copy-start(s32[16]{0:T(128)} %ref_count.3) | copy-start | bytes 196
  38.0 24.3 %collective-permute-start.10 = (bf16[4,320,128]{2,1,0:T(8,128)(2,1)S(1)}, bf16[4,320,128]{2,1,0:T(8,128)(2,1)S(1)}, u32[]{:S(2)}, u32[]{:S(2)}) collective-permute-start(bf16[4,320,128]{2,1,0:T(8,128)(2,1)S(1)} %get-tuple-element.26), channel_id=1, source_target_pairs={{0,8},{1,9},{2,10},{3,11},{4,12},{5,13},{6,14},{7,15},{8,0},{9,1},... | collective-permute-start | bytes 983048 | tf_op jit(solution)/shard_map/ppermute | solution.py:232
  41.5 25.8 %collective-permute-start.11 = (bf16[4,320,128]{2,1,0:T(8,128)(2,1)S(1)}, bf16[4,320,128]{2,1,0:T(8,128)(2,1)S(1)}, u32[]{:S(2)}, u32[]{:S(2)}) collective-permute-start(bf16[4,320,128]{2,1,0:T(8,128)(2,1)S(1)} %get-tuple-element.27), channel_id=1, source_target_pairs={{0,12},{1,13},{2,14},{3,15},{4,0},{5,1},{6,2},{7,3},{8,4},{9,5},{1... | collective-permute-start | bytes 983048 | tf_op jit(solution)/shard_map/ppermute | solution.py:232
  42.7 27.9 %collective-permute-start.9 = (bf16[4,320,128]{2,1,0:T(8,128)(2,1)S(1)}, bf16[4,320,128]{2,1,0:T(8,128)(2,1)S(1)}, u32[]{:S(2)}, u32[]{:S(2)}) collective-permute-start(bf16[4,320,128]{2,1,0:T(8,128)(2,1)S(1)} %get-tuple-element.25), channel_id=1, source_target_pairs={{0,4},{1,5},{2,6},{3,7},{4,8},{5,9},{6,10},{7,11},{8,12},{9,13},{1... | collective-permute-start | bytes 983048 | tf_op jit(solution)/shard_map/ppermute | solution.py:232

commit v4 on v3

--- a/solution.py
+++ b/solution.py
@@ -207,14 +207,26 @@
     rows, half, text_rows = plan.rows, plan.half, plan.text_rows
     slot = (place[1] * SIDE + place[2]) * text_rows + lax.broadcasted_iota(jnp.int32, (text_rows, 1), 0)
     alive = is_alive(plan, slot, owner_counts(plan, place, assign, prompt_len, ref_count))
-    for device in range(plan.shards):
-        side, shared = plan.side(device), plan.shared(device)
-        image_out[:, head(device)] = returned[device, 0:rows, :]
-        image_out[side * half : (side + 1) * half, head(shared)] = returned[device, rows : rows + half, :]
-        text = returned[device, rows + half :, :].astype(jnp.float32)
-        text_out[:, head(device)] = jnp.where(alive, text[:text_rows], 0.0).astype(text_out.dtype)
-        if side == 0:
-            text_out[:, head(shared)] = jnp.where(alive, text[text_rows:], 0.0).astype(text_out.dtype)
+    step = pl.program_id(0)
+    per = plan.shards // 2
+
+    def put(column, first, at):
+        text_out[:, head(column)] = jnp.where(alive, first[at : at + text_rows].astype(jnp.float32), 0.0).astype(text_out.dtype)
+
+    @pl.when(step < 2)
+    def _():
+        for i in range(per):
+            device = step * per + i
+            image_out[:, head(i)] = returned[device, 0:rows, :]
+            put(i, returned[device, rows + half :, :].astype(jnp.float32), 0)
+
+    @pl.when(step == 2)
+    def _():
+        for device in range(plan.shards):
+            side, column = plan.side(device), plan.shared(device) - plan.shards
+            image_out[side * half : (side + 1) * half, head(column)] = returned[device, rows : rows + half, :]
+            if side == 0:
+                put(column, returned[device, rows + half :, :].astype(jnp.float32), text_rows)
 
 
 def route(plan, place, assign, rows):
@@ -310,7 +322,11 @@
         functools.partial(unpack, plan),
         (like(rows, width), like(text_rows, width)),
         [SMEM] * 4 + [VMEM],
-        (VMEM, VMEM),
+        (
+            pl.BlockSpec((rows, width // 3), lambda i: (0, i)),
+            pl.BlockSpec((text_rows, width // 3), lambda i: (0, i)),
+        ),
+        grid=(3,),
     )(place, *lengths, returned)
     return (image_out[None], text_out[None])
 

time: 123 us -> 123 us (level)
  no operation moved by 1% of the time
where the time goes in v4:
time: 123 us
  waiting for transfers between devices  40.7 us (33%)
  starting transfers between devices  29.7 us (24%)
  blocking collectives  29.7 us (24%)
  Pallas kernels  17.3 us (14%)
  local copies, waits for them, and re-layouts  4.33 us (4%)
    ppermute x6, waiting for transfers between devices, shift(): return lax.ppermute(data, 'sp', pairs)  30.1 us
    all_to_all x1, blocking collectives, on_device(): lax.all_to_all(mixed, 'sp', split_axis=0, concat_axis=0, tiled=True)  29.7 us
    ppermute x6, starting transfers between devices, shift(): return lax.ppermute(data, 'sp', pairs)  14.2 us
    pallas_call x1, Pallas kernels, on_device(): call(functools.partial(attention, plan), like(shards, rows + half + 2 * t...  10.4 us
    all_to_all x1, waiting for transfers between devices, on_device(): whole = lax.all_to_all(whole, 'sp', split_axis=0, concat_axis=0, tiled=True)  9.6 us
    all_to_all x1, starting transfers between devices, on_device(): whole = lax.all_to_all(whole, 'sp', split_axis=0, concat_axis=0, tiled=True)  8.51 us
    ppermute x6, starting transfers between devices, exchange(): lax.ppermute(data, 'grp', [(i, i ^ bits) for i in range(plan.groups)])  7.01 us
    unnamed x20, local copies, waits for them, and re-layouts  4.33 us
  transfers between devices with their start and end apart: 13, of which 6 were waited for; matrix products, arithmetic and copies ran while one was open for 0% of the time, Pallas kernels for 4%

profile of v4, /device:TPU:32, one launch (start us, length us, event | category | flops | bytes accessed | tf_op | source)
XLA Modules:
  0.0 122.7 jit_solution(6898044506911561610)
XLA Ops:
  0.6 1.9 %collective-permute-start = (bf16[8,9216]{1,0:T(8,128)(2,1)}, bf16[8,9216]{1,0:T(8,128)(2,1)S(1)}, u32[]{:S(2)}, u32[]{:S(2)}) collective-permute-start(bf16[8,9216]{1,0:T(8,128)(2,1)} %bitcast.15), channel_id=1, source_target_pairs={{0,128},{16,144},{32,160},{48,176},{64,192},{80,208},{96,224},{112... | collective-permute-start | bytes 442376 | tf_op jit(solution)/shard_map/ppermute | solution.py:234
  2.6 0.3 collective-permute-start.2
  2.9 0.1 pad_add_fusion.place
  2.9 1.1 copy-done
  4.1 1.1 copy-done.2
  5.2 1.1 copy-done.4
  6.4 0.8 shard_map.87
  7.1 3.3 %collective-permute-start.6 = (bf16[2,384,128]{2,1,0:T(8,128)(2,1)S(1)}, bf16[2,384,128]{2,1,0:T(8,128)(2,1)S(1)}, u32[]{:S(2)}, u32[]{:S(2)}) collective-permute-start(bf16[2,384,128]{2,1,0:T(8,128)(2,1)S(1)} %get-tuple-element.20), channel_id=1, source_target_pairs={{0,1},{1,2},{2,3},{3,0},{4,5},{5,6},{6,7},{7,4},{8,9},{9,10},{10,1... | collective-permute-start | bytes 589832 | tf_op jit(solution)/shard_map/ppermute | solution.py:244
  10.5 2.2 %collective-permute-start.7 = (bf16[2,384,128]{2,1,0:T(8,128)(2,1)S(1)}, bf16[2,384,128]{2,1,0:T(8,128)(2,1)S(1)}, u32[]{:S(2)}, u32[]{:S(2)}) collective-permute-start(bf16[2,384,128]{2,1,0:T(8,128)(2,1)S(1)} %get-tuple-element.21), channel_id=1, source_target_pairs={{0,3},{1,0},{2,1},{3,2},{4,7},{5,4},{6,5},{7,6},{8,11},{9,8},{10,9... | collective-permute-start | bytes 589832 | tf_op jit(solution)/shard_map/ppermute | solution.py:244
  12.7 0.9 copy-done.6
  13.6 0.6 shard_map.86
  14.3 1.6 %collective-permute-start.3 = (bf16[8,9216]{1,0:T(8,128)(2,1)S(1)}, bf16[8,9216]{1,0:T(8,128)(2,1)S(1)}, u32[]{:S(2)}, u32[]{:S(2)}) collective-permute-start(bf16[8,9216]{1,0:T(8,128)(2,1)S(1)} %get-tuple-element.17), channel_id=1, source_target_pairs={{0,32},{16,48},{32,0},{48,16},{64,96},{80,112},{96,64},{112,80},{1... | collective-permute-start | bytes 442376 | tf_op jit(solution)/shard_map/ppermute | solution.py:234
  15.9 2.7 %collective-permute-start.4 = (bf16[8,9216]{1,0:T(8,128)(2,1)S(1)}, bf16[8,9216]{1,0:T(8,128)(2,1)S(1)}, u32[]{:S(2)}, u32[]{:S(2)}) collective-permute-start(bf16[8,9216]{1,0:T(8,128)(2,1)S(1)} %get-tuple-element.18), channel_id=1, source_target_pairs={{0,64},{16,80},{32,96},{48,112},{64,0},{80,16},{96,32},{112,48},{1... | collective-permute-start | bytes 442376 | tf_op jit(solution)/shard_map/ppermute | solution.py:234
  18.6 0.5 collective-permute-start.5
  19.1 2.8 %collective-permute-done.6.early.refs_1_ = bf16[2,384,128]{2,1,0:T(8,128)(2,1)S(1)} collective-permute-done((bf16[2,384,128]{2,1,0:T(8,128)(2,1)S(1)}, bf16[2,384,128]{2,1,0:T(8,128)(2,1)S(1)}, u32[]{:S(2)}, u32[]{:S(2)}) %collective-permute-start.6) | collective-permute-done | bytes 196640 | tf_op jit(solution)/shard_map/ppermute | solution.py:244
  21.9 3.1 %collective-permute-start.8 = (bf16[2,384,128]{2,1,0:T(8,128)(2,1)S(1)}, bf16[2,384,128]{2,1,0:T(8,128)(2,1)S(1)}, u32[]{:S(2)}, u32[]{:S(2)}) collective-permute-start(bf16[2,384,128]{2,1,0:T(8,128)(2,1)S(1)} %get-tuple-element.23), channel_id=1, source_target_pairs={{0,2},{1,3},{2,0},{3,1},{4,6},{5,7},{6,4},{7,5},{8,10},{9,11},{10,... | collective-permute-start | bytes 589832 | tf_op jit(solution)/shard_map/ppermute | solution.py:244
  25.0 1.5 %shard_map.88.whole = bf16[16,432,128]{2,1,0:T(8,128)(2,1)} custom-call(bf16[128,3072]{1,0:T(8,128)(2,1)S(1)} %bitcast.10, bf16[128,3072]{1,0:T(8,128)(2,1)S(1)} %bitcast.12, bf16[128,3072]{1,0:T(8,128)(2,1)S(1)} %bitcast.14), custom_call_target="tpu_custom_call" | custom-call | tf_op jit(solution)/shard_map/pallas_call | solution.py:291
  26.5 1.0 collective-permute-done.5.h6
  27.5 1.3 %shard_map.89 = bf16[16,432,128]{2,1,0:T(8,128)(2,1)} custom-call(s32[3]{0:T(128)S(1)} %pad_add_fusion.place, s32[16]{0:T(128)S(1)} %copy-done.7, bf16[8,9216]{1,0:T(8,128)(2,1)S(1)} %get-tuple-element.16.h0, bf16[8,9216]{1,0:T(8,128)(2,1)S(1)} %collective-permute-done.3.h2, ...), custom_call_target="tpu_custom_call", output_to_operand_aliasing={{}: (8, {})} | custom-call | tf_op jit(solution)/shard_map/pallas_call | solution.py:300
  28.8 8.5 %all-to-all-start = ((bf16[16,432,128]{2,1,0:T(8,128)(2,1)}), bf16[16,432,128]{2,1,0:T(8,128)(2,1)S(1)}, u32[]{:S(2)}, u32[]{:S(2)}) async-start(bf16[16,432,128]{2,1,0:T(8,128)(2,1)} %shard_map.89), calls=%async_computation | async-start | bytes 3538944 | tf_op jit(solution)/shard_map/all_to_all | solution.py:308
  37.3 0.0 copy-start.8
  37.3 0.6 shard_map.90
  38.0 3.5 %collective-permute-start.10 = (bf16[4,320,128]{2,1,0:T(8,128)(2,1)S(1)}, bf16[4,320,128]{2,1,0:T(8,128)(2,1)S(1)}, u32[]{:S(2)}, u32[]{:S(2)}) collective-permute-start(bf16[4,320,128]{2,1,0:T(8,128)(2,1)S(1)} %get-tuple-element.26), channel_id=1, source_target_pairs={{0,8},{1,9},{2,10},{3,11},{4,12},{5,13},{6,14},{7,15},{8,0},{9,1},... | collective-permute-start | bytes 983048 | tf_op jit(solution)/shard_map/ppermute | solution.py:244
  41.5 1.2 collective-permute-start.11
  42.6 0.9 collective-permute-start.9
  43.5 20.4 %collective-permute-done.10.p2 = bf16[4,320,128]{2,1,0:T(8,128)(2,1)S(1)} collective-permute-done((bf16[4,320,128]{2,1,0:T(8,128)(2,1)S(1)}, bf16[4,320,128]{2,1,0:T(8,128)(2,1)S(1)}, u32[]{:S(2)}, u32[]{:S(2)}) %collective-permute-start.10) | collective-permute-done | bytes 327712 | tf_op jit(solution)/shard_map/ppermute | solution.py:244
  63.9 6.6 %collective-permute-done.11.p3 = bf16[4,320,128]{2,1,0:T(8,128)(2,1)S(1)} collective-permute-done((bf16[4,320,128]{2,1,0:T(8,128)(2,1)S(1)}, bf16[4,320,128]{2,1,0:T(8,128)(2,1)S(1)}, u32[]{:S(2)}, u32[]{:S(2)}) %collective-permute-start.11) | collective-permute-done | bytes 327712 | tf_op jit(solution)/shard_map/ppermute | solution.py:244
  70.5 0.3 collective-permute-done.9.p1
  70.8 9.6 %all-to-all-done.came = bf16[16,432,128]{2,1,0:T(8,128)(2,1)S(1)} async-done(((bf16[16,432,128]{2,1,0:T(8,128)(2,1)}), bf16[16,432,128]{2,1,0:T(8,128)(2,1)S(1)}, u32[]{:S(2)}, u32[]{:S(2)}) %all-to-all-start) | async-done | bytes 1769504 | tf_op jit(solution)/shard_map/all_to_all | solution.py:308
  80.4 10.4 %shard_map.91 = bf16[16,208,128]{2,1,0:T(8,128)(2,1)S(1)} custom-call(s32[3]{0:T(128)S(1)} %pad_add_fusion.place, s32[16]{0:T(128)S(1)} %copy-done.7, s32[16]{0:T(128)S(1)} %copy-done.8, s32[16]{0:T(128)S(1)} %copy-done.9, bf16[16,432,128]{2,1,0:T(8,128)(2,1)S(1)} %all-to-all-done.came, bf16[4,320,128]{2,1,0:T(8,128)(2,1)S(1)} %get-tuple-element.24.p0, ...), custom_call_target="tpu_custom_call" | custom-call | tf_op jit(solution)/shard_map/pallas_call | solution.py:311
  90.8 29.7 %all_to_all.10.returned = bf16[16,208,128]{2,1,0:T(8,128)(2,1)S(1)} all-to-all(bf16[16,208,128]{2,1,0:T(8,128)(2,1)S(1)} %shard_map.91), channel_id=1, replica_groups=mesh['grp'=16,'sp'=16] {'sp'}, dimensions={0} | all-to-all | bytes 1703936 | tf_op jit(solution)/shard_map/all_to_all | solution.py:320
  120.5 2.2 %shard_map.92 = (bf16[128,3072]{1,0:T(8,128)(2,1)}, bf16[8,3072]{1,0:T(8,128)(2,1)}) custom-call(s32[3]{0:T(128)S(1)} %pad_add_fusion.place, s32[16]{0:T(128)S(1)} %copy-done.7, s32[16]{0:T(128)S(1)} %copy-done.8, s32[16]{0:T(128)S(1)} %copy-done.9, bf16[16,208,128]{2,1,0:T(8,128)(2,1)S(1)} %all_to_all.10.returned), custom_call_target="tpu_custom_call" | custom-call | tf_op jit(solution)/shard_map/pallas_call | solution.py:321
  (23 shorter events, 0.1 us)
Async XLA Ops:
  0.6 12.1 %copy-start.7 = (s32[16]{0:T(128)S(1)}, s32[16]{0:T(128)}, u32[]{:S(2)}) copy-start(s32[16]{0:T(128)} %assign.7) | copy-start | bytes 196
  0.6 12.0 %collective-permute-start = (bf16[8,9216]{1,0:T(8,128)(2,1)}, bf16[8,9216]{1,0:T(8,128)(2,1)S(1)}, u32[]{:S(2)}, u32[]{:S(2)}) collective-permute-start(bf16[8,9216]{1,0:T(8,128)(2,1)} %bitcast.15), channel_id=1, source_target_pairs={{0,128},{16,144},{32,160},{48,176},{64,192},{80,208},{96,224},{112... | collective-permute-start | bytes 442376 | tf_op jit(solution)/shard_map/ppermute | solution.py:234
  2.6 10.1 %collective-permute-start.1 = (bf16[8,9216]{1,0:T(8,128)(2,1)}, bf16[8,9216]{1,0:T(8,128)(2,1)S(1)}, u32[]{:S(2)}, u32[]{:S(2)}) collective-permute-start(bf16[8,9216]{1,0:T(8,128)(2,1)} %bitcast.16), channel_id=1, source_target_pairs={{0,16},{16,0},{32,48},{48,32},{64,80},{80,64},{96,112},{112,96},{1... | collective-permute-start | bytes 442376 | tf_op jit(solution)/shard_map/ppermute | solution.py:234
  2.6 10.1 %collective-permute-start.2 = (bf16[8,9216]{1,0:T(8,128)(2,1)}, bf16[8,9216]{1,0:T(8,128)(2,1)S(1)}, u32[]{:S(2)}, u32[]{:S(2)}) collective-permute-start(bf16[8,9216]{1,0:T(8,128)(2,1)} %bitcast.17), channel_id=1, source_target_pairs={{0,144},{16,128},{32,176},{48,160},{64,208},{80,192},{96,240},{112... | collective-permute-start | bytes 442376 | tf_op jit(solution)/shard_map/ppermute | solution.py:234
  2.9 1.1 copy-start
  4.1 1.1 copy-start.2
  5.2 1.1 copy-start.4
  6.3 18.6 %copy-start.1 = (bf16[1,128,3072]{2,1,0:T(8,128)(2,1)S(1)}, bf16[1,128,3072]{2,1,0:T(8,128)(2,1)}, u32[]{:S(2)}) copy-start(bf16[1,128,3072]{2,1,0:T(8,128)(2,1)} %param.7) | copy-start | bytes 2359300
  6.3 18.6 %copy-start.3 = (bf16[1,128,3072]{2,1,0:T(8,128)(2,1)S(1)}, bf16[1,128,3072]{2,1,0:T(8,128)(2,1)}, u32[]{:S(2)}) copy-start(bf16[1,128,3072]{2,1,0:T(8,128)(2,1)} %param.8) | copy-start | bytes 2359300
  6.4 18.6 %copy-start.5 = (bf16[1,128,3072]{2,1,0:T(8,128)(2,1)S(1)}, bf16[1,128,3072]{2,1,0:T(8,128)(2,1)}, u32[]{:S(2)}) copy-start(bf16[1,128,3072]{2,1,0:T(8,128)(2,1)} %param.9) | copy-start | bytes 2359300
  7.1 14.8 %collective-permute-start.6 = (bf16[2,384,128]{2,1,0:T(8,128)(2,1)S(1)}, bf16[2,384,128]{2,1,0:T(8,128)(2,1)S(1)}, u32[]{:S(2)}, u32[]{:S(2)}) collective-permute-start(bf16[2,384,128]{2,1,0:T(8,128)(2,1)S(1)} %get-tuple-element.20), channel_id=1, source_target_pairs={{0,1},{1,2},{2,3},{3,0},{4,5},{5,6},{6,7},{7,4},{8,9},{9,10},{10,1... | collective-permute-start | bytes 589832 | tf_op jit(solution)/shard_map/ppermute | solution.py:244
  10.5 16.0 %collective-permute-start.7 = (bf16[2,384,128]{2,1,0:T(8,128)(2,1)S(1)}, bf16[2,384,128]{2,1,0:T(8,128)(2,1)S(1)}, u32[]{:S(2)}, u32[]{:S(2)}) collective-permute-start(bf16[2,384,128]{2,1,0:T(8,128)(2,1)S(1)} %get-tuple-element.21), channel_id=1, source_target_pairs={{0,3},{1,0},{2,1},{3,2},{4,7},{5,4},{6,5},{7,6},{8,11},{9,8},{10,9... | collective-permute-start | bytes 589832 | tf_op jit(solution)/shard_map/ppermute | solution.py:244
  12.7 0.9 copy-start.6
  14.3 12.2 %collective-permute-start.3 = (bf16[8,9216]{1,0:T(8,128)(2,1)S(1)}, bf16[8,9216]{1,0:T(8,128)(2,1)S(1)}, u32[]{:S(2)}, u32[]{:S(2)}) collective-permute-start(bf16[8,9216]{1,0:T(8,128)(2,1)S(1)} %get-tuple-element.17), channel_id=1, source_target_pairs={{0,32},{16,48},{32,0},{48,16},{64,96},{80,112},{96,64},{112,80},{1... | collective-permute-start | bytes 442376 | tf_op jit(solution)/shard_map/ppermute | solution.py:234
  15.9 10.6 %collective-permute-start.4 = (bf16[8,9216]{1,0:T(8,128)(2,1)S(1)}, bf16[8,9216]{1,0:T(8,128)(2,1)S(1)}, u32[]{:S(2)}, u32[]{:S(2)}) collective-permute-start(bf16[8,9216]{1,0:T(8,128)(2,1)S(1)} %get-tuple-element.18), channel_id=1, source_target_pairs={{0,64},{16,80},{32,96},{48,112},{64,0},{80,16},{96,32},{112,48},{1... | collective-permute-start | bytes 442376 | tf_op jit(solution)/shard_map/ppermute | solution.py:234
  18.6 8.9 %collective-permute-start.5 = (bf16[8,9216]{1,0:T(8,128)(2,1)S(1)}, bf16[8,9216]{1,0:T(8,128)(2,1)S(1)}, u32[]{:S(2)}, u32[]{:S(2)}) collective-permute-start(bf16[8,9216]{1,0:T(8,128)(2,1)S(1)} %get-tuple-element.19), channel_id=1, source_target_pairs={{0,96},{16,112},{32,64},{48,80},{64,32},{80,48},{96,0},{112,16},{1... | collective-permute-start | bytes 442376 | tf_op jit(solution)/shard_map/ppermute | solution.py:234
  21.9 15.4 %collective-permute-start.8 = (bf16[2,384,128]{2,1,0:T(8,128)(2,1)S(1)}, bf16[2,384,128]{2,1,0:T(8,128)(2,1)S(1)}, u32[]{:S(2)}, u32[]{:S(2)}) collective-permute-start(bf16[2,384,128]{2,1,0:T(8,128)(2,1)S(1)} %get-tuple-element.23), channel_id=1, source_target_pairs={{0,2},{1,3},{2,0},{3,1},{4,6},{5,7},{6,4},{7,5},{8,10},{9,11},{10,... | collective-permute-start | bytes 589832 | tf_op jit(solution)/shard_map/ppermute | solution.py:244
  28.8 51.6 %all-to-all-start = ((bf16[16,432,128]{2,1,0:T(8,128)(2,1)}), bf16[16,432,128]{2,1,0:T(8,128)(2,1)S(1)}, u32[]{:S(2)}, u32[]{:S(2)}) async-start(bf16[16,432,128]{2,1,0:T(8,128)(2,1)} %shard_map.89), calls=%async_computation | async-start | bytes 3538944 | tf_op jit(solution)/shard_map/all_to_all | solution.py:308
  37.3 43.1 %copy-start.8 = (s32[16]{0:T(128)S(1)}, s32[16]{0:T(128)}, u32[]{:S(2)}) copy-start(s32[16]{0:T(128)} %prompt_len.3) | copy-start | bytes 196
  37.3 43.1 %copy-start.9 = (s32[16]{0:T(128)S(1)}, s32[16]{0:T(128)}, u32[]{:S(2)}) copy-start(s32[16]{0:T(128)} %ref_count.3) | copy-start | bytes 196
  38.0 25.9 %collective-permute-start.10 = (bf16[4,320,128]{2,1,0:T(8,128)(2,1)S(1)}, bf16[4,320,128]{2,1,0:T(8,128)(2,1)S(1)}, u32[]{:S(2)}, u32[]{:S(2)}) collective-permute-start(bf16[4,320,128]{2,1,0:T(8,128)(2,1)S(1)} %get-tuple-element.26), channel_id=1, source_target_pairs={{0,8},{1,9},{2,10},{3,11},{4,12},{5,13},{6,14},{7,15},{8,0},{9,1},... | collective-permute-start | bytes 983048 | tf_op jit(solution)/shard_map/ppermute | solution.py:244
  41.5 29.0 %collective-permute-start.11 = (bf16[4,320,128]{2,1,0:T(8,128)(2,1)S(1)}, bf16[4,320,128]{2,1,0:T(8,128)(2,1)S(1)}, u32[]{:S(2)}, u32[]{:S(2)}) collective-permute-start(bf16[4,320,128]{2,1,0:T(8,128)(2,1)S(1)} %get-tuple-element.27), channel_id=1, source_target_pairs={{0,12},{1,13},{2,14},{3,15},{4,0},{5,1},{6,2},{7,3},{8,4},{9,5},{1... | collective-permute-start | bytes 983048 | tf_op jit(solution)/shard_map/ppermute | solution.py:244
  42.6 28.2 %collective-permute-start.9 = (bf16[4,320,128]{2,1,0:T(8,128)(2,1)S(1)}, bf16[4,320,128]{2,1,0:T(8,128)(2,1)S(1)}, u32[]{:S(2)}, u32[]{:S(2)}) collective-permute-start(bf16[4,320,128]{2,1,0:T(8,128)(2,1)S(1)} %get-tuple-element.25), channel_id=1, source_target_pairs={{0,4},{1,5},{2,6},{3,7},{4,8},{5,9},{6,10},{7,11},{8,12},{9,13},{1... | collective-permute-start | bytes 983048 | tf_op jit(solution)/shard_map/ppermute | solution.py:244
